TPU v7x, 32 devices: a whole 2x2x4 slice. The times are simulated.
32 devices in a mesh: dp: 16 (over z, y, x), tensor: 2 (over core).
Axes of the slice: x: 2, y: 2, z: 4, core: 2. Of those that a mesh axis runs over, the one named last changes fastest.
Arguments:
- inputs: bfloat16 [16384, 1024], P(('dp', 'tensor')), may hold values from -6 to 6
- segments: int32 [16384], P('dp'), may hold values from 0 to 16383, as said below
- cotangent: bfloat16 [16384, 1024], P(('dp', 'tensor')), may hold values from -6 to 6
- norm_gain: bfloat16 [1024], P(('dp', 'tensor')), may hold values from 0.5 to 1.5
- mix_in: bfloat16 [1024, 24, 128], P('dp', 'tensor'), may hold values from -0.1875 to 0.1875
- step_in: bfloat16 [1024, 24], P('dp', 'tensor'), may hold values from -0.1875 to 0.1875
- state_in: bfloat16 [1024, 256], P(('dp', 'tensor')), may hold values from -0.1875 to 0.1875
- conv_inner: bfloat16 [4, 1536], P(None, ('dp', 'tensor')), may hold values from -3 to 3
- conv_inner_bias: bfloat16 [1536], P(('dp', 'tensor')), may hold values from -1.5 to 1.5
- conv_state: bfloat16 [4, 256], P(None, ('dp', 'tensor')), may hold values from -3 to 3
- conv_state_bias: bfloat16 [256], P(('dp', 'tensor')), may hold values from -1.5 to 1.5
- decay_log: float32 [24], P('tensor'), may hold values from 0 to 2.7
- step_bias: float32 [24], P('tensor'), may hold values from -6 to -2
- skip_gain: float32 [24], P('tensor'), may hold values from 0.5 to 1.5
- mixer_gain: bfloat16 [1536], P(('dp', 'tensor')), may hold values from 0.5 to 1.5
- attn_in: bfloat16 [1024, 2, 384], P('dp', 'tensor'), may hold values from -0.1875 to 0.1875
- mixer_out: bfloat16 [24, 64, 1024], P('tensor', None, 'dp'), may hold values from -0.15625 to 0.15625
- attn_out: bfloat16 [2, 256, 1024], P('tensor', None, 'dp'), may hold values from -3 to 3
- ffn_gain: bfloat16 [1024], P(('dp', 'tensor')), may hold values from 0.5 to 1.5
- ffn_in: bfloat16 [1024, 2, 2048], P('dp', None, 'tensor'), may hold values from -0.1875 to 0.1875
- ffn_down: bfloat16 [2048, 1024], P('tensor', 'dp'), may hold values from -0.125 to 0.125
Outputs:
- output: bfloat16 [16384, 1024], P(('dp', 'tensor'))
- inputs_grad: float32 [16384, 1024], P(('dp', 'tensor'))
- norm_gain_grad: float32 [1024], P(('dp', 'tensor'))
- mix_in_grad: float32 [1024, 24, 128], P('dp', 'tensor')
- step_in_grad: float32 [1024, 24], P('dp', 'tensor')
- state_in_grad: float32 [1024, 256], P(('dp', 'tensor'))
- conv_inner_grad: float32 [4, 1536], P(None, ('dp', 'tensor'))
- conv_inner_bias_grad: float32 [1536], P(('dp', 'tensor'))
- conv_state_grad: float32 [4, 256], P(None, ('dp', 'tensor'))
- conv_state_bias_grad: float32 [256], P(('dp', 'tensor'))
- decay_log_grad: float32 [24], P('tensor')
- step_bias_grad: float32 [24], P('tensor')
- skip_gain_grad: float32 [24], P('tensor')
- mixer_gain_grad: float32 [1536], P(('dp', 'tensor'))
- attn_in_grad: float32 [1024, 2, 384], P('dp', 'tensor')
- mixer_out_grad: float32 [24, 64, 1024], P('tensor', None, 'dp')
- attn_out_grad: float32 [2, 256, 1024], P('tensor', None, 'dp')
- ffn_gain_grad: float32 [1024], P(('dp', 'tensor'))
- ffn_in_grad: float32 [1024, 2, 2048], P('dp', None, 'tensor')
- ffn_down_grad: float32 [2048, 1024], P('tensor', 'dp')
Inputs may be any that keep to these rules, and one draw needn't show every extreme that they name: `segments`: each token's segment number is the index of its document's first token, so numbers never fall; every sequence of 1024 tokens begins a new document, the last token of all is a document of its own, and tokens 512 - 1 and 512 of a sequence lie in one document.
All inputs are finite; a program needn't handle non-finite values.
Results may differ from a plain program's by a relative error of at most 0.014.
Values may be sent and summed in bfloat16 or wider, within the bound.
A program may use at most 192 MiB of HBM per device.

v0:
```python
import jax
import jax.numpy as jnp
from jax import lax
from jax.sharding import PartitionSpec as P

QPK = 4
ADIM = 64
NGH = 12
BLK = 256


HIGH = lax.Precision.HIGHEST
EPS = 1e-05
ROPE_BASE = 100000000000.0


def positions(segment):
    index = jnp.arange(segment.shape[0], dtype=jnp.int32)
    fresh = jnp.concatenate([jnp.ones((1,), dtype=bool), segment[1:] != segment[:-1]])
    starting = lax.cummax(jnp.where(fresh, index, jnp.zeros_like(index)), axis=0)
    return index - starting


def rotate(values, places, direction):
    half_dim = values.shape[-1] // 2
    freqs = ROPE_BASE ** (-2.0 * jnp.arange(half_dim, dtype=jnp.float32) / values.shape[-1])
    angles = places.astype(jnp.float32)[:, None] * freqs[None, :]
    bshape = (values.shape[0],) + (1,) * (values.ndim - 2) + (half_dim,)
    cosine = jnp.cos(angles).reshape(bshape)
    sine = direction * jnp.sin(angles).reshape(bshape)
    first_half = values[..., :half_dim]
    second_half = values[..., half_dim:]
    return jnp.concatenate(
        [first_half * cosine - second_half * sine, second_half * cosine + first_half * sine], -1
    )


def seg_conv(values, taps, shift_bias, segment):
    n_rows = values.shape[0]
    n_taps = taps.shape[0]
    padded = jnp.pad(values, ((n_taps - 1, 0), (0, 0)))
    seg_pad = jnp.concatenate([jnp.full((n_taps - 1,), -1, dtype=jnp.int32), segment])
    result = jnp.zeros_like(values) + shift_bias[None, :]
    for offset in range(n_taps):
        same_doc = (seg_pad[offset : offset + n_rows] == segment).astype(values.dtype)
        result = (
            result + taps[offset][None, :] * padded[offset : offset + n_rows] * same_doc[:, None]
        )
    return result


def ssd_scan(inner, steps, decays, b_state, c_state, segment, block_len):
    n_rows, n_heads, head_dim = inner.shape
    n_blocks = n_rows // block_len
    x_blk = inner.reshape(n_blocks, block_len, n_heads, head_dim)
    dt_blk = steps.reshape(n_blocks, block_len, n_heads)
    cumul = jnp.cumsum(decays.reshape(n_blocks, block_len, n_heads), axis=1)
    b_blk = b_state.reshape(n_blocks, block_len, -1)
    c_blk = c_state.reshape(n_blocks, block_len, -1)
    seg_blk = segment.reshape(n_blocks, block_len)
    within = jnp.arange(block_len, dtype=jnp.int32)
    causal = within[:, None] >= within[None, :]
    allowed = (seg_blk[:, :, None] == seg_blk[:, None, :]) & causal[None]
    differ = cumul[:, :, None, :] - cumul[:, None, :, :]
    kernel = jnp.exp(jnp.where(allowed[..., None], differ, -1e30))
    inner_prod = jnp.einsum("ctn,csn->cts", c_blk, b_blk, precision=HIGH)
    weights_ts = inner_prod[..., None] * kernel * dt_blk[:, None, :, :]
    y_inner = jnp.einsum("ctsh,cshp->cthp", weights_ts, x_blk, precision=HIGH)
    last_seg = seg_blk[:, -1]
    to_end = (
        jnp.exp(cumul[:, -1:, :] - cumul)
        * (seg_blk == last_seg[:, None]).astype(inner.dtype)[..., None]
    )
    local_state = jnp.einsum("csh,cshp,csn->chpn", to_end * dt_blk, x_blk, b_blk, precision=HIGH)
    prev_seg = jnp.concatenate([jnp.full((1,), -1, dtype=jnp.int32), last_seg[:-1]])
    carry_keep = jnp.exp(cumul[:, -1, :]) * (last_seg == prev_seg).astype(inner.dtype)[:, None]

    def advance(state, items):
        keep_row, fresh_state = items
        return (state * keep_row[:, None, None] + fresh_state, state)

    zero_state = jnp.zeros(local_state.shape[1:], inner.dtype)
    final_state, entering = lax.scan(advance, zero_state, (carry_keep, local_state))
    from_start = jnp.exp(cumul) * (seg_blk == prev_seg[:, None]).astype(inner.dtype)[..., None]
    y_state = jnp.einsum("ctn,chpn->cthp", c_blk, entering, precision=HIGH) * from_start[..., None]
    return (y_inner + y_state).reshape(n_rows, n_heads, head_dim)


def mamba_core(
    proj_zx,
    proj_step,
    proj_bc,
    conv_w,
    conv_b,
    conv_s,
    conv_sb,
    log_decay,
    bias_step,
    gain_skip,
    gain_mix,
    segment,
    block_len,
    group_heads,
):
    n_rows, n_heads, twice = proj_zx.shape
    head_dim = twice // 2
    gate_z = proj_zx[..., :head_dim]
    x_conv = jax.nn.silu(
        seg_conv(
            proj_zx[..., head_dim:].reshape(n_rows, n_heads * head_dim), conv_w, conv_b, segment
        )
    )
    inner = x_conv.reshape(n_rows, n_heads, head_dim)
    bc_conv = jax.nn.silu(seg_conv(proj_bc, conv_s, conv_sb, segment))
    n_state = proj_bc.shape[1] // 2
    steps = jax.nn.softplus(proj_step + bias_step[None, :])
    decays = -steps * jnp.exp(log_decay)[None, :]
    ssm = ssd_scan(
        inner, steps, decays, bc_conv[:, :n_state], bc_conv[:, n_state:], segment, block_len
    )
    ssm = ssm + gain_skip[None, :, None] * inner
    gated = ssm * jax.nn.silu(gate_z)
    grouped = gated.reshape(n_rows, n_heads // group_heads, group_heads * head_dim)
    grouped = grouped * lax.rsqrt(jnp.mean(grouped * grouped, -1, keepdims=True) + EPS)
    return grouped.reshape(n_rows, n_heads * head_dim) * gain_mix[None, :]


def masked_scores(q_blk, keys, seg_q, place_q, segment, scaling):
    scores = jnp.einsum("tgqd,sgd->gqts", q_blk, keys, preferred_element_type=jnp.float32) * scaling
    key_places = jnp.arange(segment.shape[0], dtype=jnp.int32)
    allowed = (seg_q[:, None] == segment[None, :]) & (place_q[:, None] >= key_places[None, :])
    return jnp.where(allowed[None, None], scores, -1e30)


def attend_forward(queries, keys, vals, segment, q_len, scaling):
    n_rows = segment.shape[0]
    n_q = n_rows // q_len
    row_index = jnp.arange(n_rows, dtype=jnp.int32)

    def one_block(block_items):
        q_blk, seg_q, place_q = block_items
        scores = masked_scores(q_blk, keys, seg_q, place_q, segment, scaling)
        topmost = jnp.max(scores, -1, keepdims=True)
        expo = jnp.exp(scores - topmost)
        total = jnp.sum(expo, -1, keepdims=True)
        probs = (expo / total).astype(jnp.bfloat16)
        attended = jnp.einsum("gqts,sgd->tgqd", probs, vals, preferred_element_type=jnp.float32)
        return (attended, (topmost + jnp.log(total))[..., 0])

    attended, log_norm = lax.map(
        one_block,
        (
            queries.reshape((n_q, q_len) + queries.shape[1:]),
            segment.reshape(n_q, q_len),
            row_index.reshape(n_q, q_len),
        ),
    )
    return (attended.reshape(queries.shape), log_norm)


def attend_backward(queries, keys, vals, segment, log_norm, grad_out, q_len, scaling):
    n_rows = segment.shape[0]
    n_q = n_rows // q_len
    row_index = jnp.arange(n_rows, dtype=jnp.int32)

    def one_block(carry, block_items):
        grad_keys, grad_vals = carry
        q_blk, seg_q, place_q, norm_blk, dout_blk = block_items
        scores = masked_scores(q_blk, keys, seg_q, place_q, segment, scaling)
        probs = jnp.exp(scores - norm_blk[..., None])
        probs_low = probs.astype(jnp.bfloat16)
        grad_vals = grad_vals + jnp.einsum(
            "gqts,tgqd->sgd", probs_low, dout_blk, preferred_element_type=jnp.float32
        )
        grad_probs = jnp.einsum(
            "tgqd,sgd->gqts", dout_blk, vals, preferred_element_type=jnp.float32
        )
        grad_scores = probs * (grad_probs - jnp.sum(probs * grad_probs, -1, keepdims=True))
        scores_low = grad_scores.astype(jnp.bfloat16)
        grad_q = (
            jnp.einsum("gqts,sgd->tgqd", scores_low, keys, preferred_element_type=jnp.float32)
            * scaling
        )
        grad_keys = (
            grad_keys
            + jnp.einsum("gqts,tgqd->sgd", scores_low, q_blk, preferred_element_type=jnp.float32)
            * scaling
        )
        return ((grad_keys, grad_vals), grad_q)

    empty = jnp.zeros(keys.shape, jnp.float32)
    sums, grad_q = lax.scan(
        one_block,
        (empty, empty),
        (
            queries.reshape((n_q, q_len) + queries.shape[1:]),
            segment.reshape(n_q, q_len),
            row_index.reshape(n_q, q_len),
            log_norm,
            grad_out.reshape((n_q, q_len) + grad_out.shape[1:]),
        ),
    )
    return (grad_q.reshape(queries.shape), sums[0], sums[1])


def norm_back(grad_normed, unit_rows, inv_scale, gain):
    scaled = grad_normed * gain[None, :]
    return inv_scale * (scaled - unit_rows * jnp.mean(scaled * unit_rows, -1, keepdims=True))


def per_device(
    inputs,
    segments,
    cotangent,
    norm_gain,
    mix_in,
    step_in,
    state_in,
    conv_inner,
    conv_inner_bias,
    conv_state,
    conv_state_bias,
    decay_log,
    step_bias,
    skip_gain,
    mixer_gain,
    attn_in,
    mixer_out,
    attn_out,
    ffn_gain,
    ffn_in,
    ffn_down,
):
    full_mix, full_step, full_attn, full_mixout, full_attnout, full_ffin, full_down = (
        lax.all_gather(mix_in, "dp", axis=0, tiled=True),
        lax.all_gather(step_in, "dp", axis=0, tiled=True),
        lax.all_gather(attn_in, "dp", axis=0, tiled=True),
        lax.all_gather(mixer_out, "dp", axis=2, tiled=True),
        lax.all_gather(attn_out, "dp", axis=2, tiled=True),
        lax.all_gather(ffn_in, "dp", axis=0, tiled=True),
        lax.all_gather(ffn_down, "dp", axis=1, tiled=True),
    )
    smalls = (
        lax.all_gather(norm_gain, ("dp", "tensor"), axis=0, tiled=True),
        lax.all_gather(ffn_gain, ("dp", "tensor"), axis=0, tiled=True),
        lax.all_gather(state_in, ("dp", "tensor"), axis=0, tiled=True),
        lax.all_gather(conv_inner, ("dp", "tensor"), axis=1, tiled=True),
        lax.all_gather(conv_inner_bias, ("dp", "tensor"), axis=0, tiled=True),
        lax.all_gather(mixer_gain, ("dp", "tensor"), axis=0, tiled=True),
        lax.all_gather(conv_state, ("dp", "tensor"), axis=1, tiled=True),
        lax.all_gather(conv_state_bias, ("dp", "tensor"), axis=0, tiled=True),
    )
    part = lax.axis_index("tensor")
    n_parts = lax.axis_size("tensor")
    inner_cols = smalls[3].shape[1] // n_parts

    def local_cols(array, axis_dim):
        return lax.dynamic_slice_in_dim(array, part * inner_cols, inner_cols, axis_dim).astype(
            jnp.float32
        )

    def widen(local, axis_dim):
        full_shape = list(local.shape)
        full_shape[axis_dim] = inner_cols * n_parts
        return lax.dynamic_update_slice_in_dim(
            jnp.zeros(full_shape, jnp.float32), local, part * inner_cols, axis_dim
        )

    gain_first = smalls[0].astype(jnp.float32)
    gain_second = smalls[1].astype(jnp.float32)
    full_state = smalls[2]
    conv_local = local_cols(smalls[3], 1)
    conv_bias_local = local_cols(smalls[4], 0)
    gain_mixer = local_cols(smalls[5], 0)
    conv_bc = smalls[6].astype(jnp.float32)
    conv_bc_bias = smalls[7].astype(jnp.float32)
    inputs_f = inputs.astype(jnp.float32)
    inv_first = lax.rsqrt(jnp.mean(inputs_f * inputs_f, -1, keepdims=True) + EPS)
    unit_first = inputs_f * inv_first
    normed = lax.all_gather(
        (unit_first * gain_first[None, :]).astype(jnp.bfloat16), "tensor", axis=0, tiled=True
    )
    proj_zx = jnp.einsum("td,dhc->thc", normed, full_mix, preferred_element_type=jnp.float32)
    proj_step = jnp.einsum("td,dh->th", normed, full_step, preferred_element_type=jnp.float32)
    proj_bc = jnp.einsum("td,dn->tn", normed, full_state, preferred_element_type=jnp.float32)
    proj_qkv = jnp.einsum("td,dgc->tgc", normed, full_attn, preferred_element_type=jnp.float32)

    def mixer(
        zx_in,
        raw_in,
        bc_in,
        conv_w,
        conv_b,
        conv_s,
        conv_sb,
        log_decay,
        bias_step,
        gain_skip,
        gain_mix,
    ):
        return mamba_core(
            zx_in,
            raw_in,
            bc_in,
            conv_w,
            conv_b,
            conv_s,
            conv_sb,
            log_decay,
            bias_step,
            gain_skip,
            gain_mix,
            segments,
            BLK,
            NGH,
        )

    mamba_value, mamba_pull = jax.vjp(
        mixer,
        proj_zx,
        proj_step,
        proj_bc,
        conv_local,
        conv_bias_local,
        conv_bc,
        conv_bc_bias,
        decay_log,
        step_bias,
        skip_gain,
        gain_mixer,
    )
    n_rows = segments.shape[0]
    n_heads = proj_zx.shape[1]
    mamba_low = mamba_value.reshape(n_rows, n_heads, -1).astype(jnp.bfloat16)
    mamba_part = jnp.einsum(
        "thc,hcd->td", mamba_low, full_mixout, preferred_element_type=jnp.float32
    )
    places = positions(segments)
    groups = proj_qkv.shape[1]
    q_len = min(512, n_rows)
    scaling = ADIM ** (-0.5)
    q_part = proj_qkv[..., : QPK * ADIM].reshape(n_rows, groups, QPK, ADIM)
    queries = rotate(q_part, places, 1.0).astype(jnp.bfloat16)
    keys = rotate(proj_qkv[..., QPK * ADIM : (QPK + 1) * ADIM], places, 1.0).astype(jnp.bfloat16)
    vals = proj_qkv[..., (QPK + 1) * ADIM :].astype(jnp.bfloat16)
    attended, log_norm = attend_forward(queries, keys, vals, segments, q_len, scaling)
    attended_low = attended.reshape(n_rows, groups, QPK * ADIM).astype(jnp.bfloat16)
    attn_part = jnp.einsum(
        "tgc,gcd->td", attended_low, full_attnout, preferred_element_type=jnp.float32
    )
    mixed = lax.psum_scatter(mamba_part + attn_part, "tensor", scatter_dimension=0, tiled=True)
    middle = inputs_f + mixed
    inv_second = lax.rsqrt(jnp.mean(middle * middle, -1, keepdims=True) + EPS)
    unit_second = middle * inv_second
    hidden = lax.all_gather(
        (unit_second * gain_second[None, :]).astype(jnp.bfloat16), "tensor", axis=0, tiled=True
    )
    gate_up = jnp.einsum("td,dkf->tkf", hidden, full_ffin, preferred_element_type=jnp.float32)
    gate = gate_up[:, 0]
    upper = gate_up[:, 1]
    sigma = jax.nn.sigmoid(gate)
    active = (gate * sigma * upper).astype(jnp.bfloat16)
    ffn_part = jnp.einsum("tf,fd->td", active, full_down, preferred_element_type=jnp.float32)
    ffn_value = lax.psum_scatter(
        ffn_part.astype(jnp.bfloat16), "tensor", scatter_dimension=0, tiled=True
    ).astype(jnp.float32)
    output = (middle + ffn_value).astype(jnp.bfloat16)
    full_mix, full_step, full_attn, full_mixout, full_attnout, full_ffin, full_down = (
        lax.all_gather(mix_in, "dp", axis=0, tiled=True),
        lax.all_gather(step_in, "dp", axis=0, tiled=True),
        lax.all_gather(attn_in, "dp", axis=0, tiled=True),
        lax.all_gather(mixer_out, "dp", axis=2, tiled=True),
        lax.all_gather(attn_out, "dp", axis=2, tiled=True),
        lax.all_gather(ffn_in, "dp", axis=0, tiled=True),
        lax.all_gather(ffn_down, "dp", axis=1, tiled=True),
    )
    cot_full = lax.all_gather(cotangent, "tensor", axis=0, tiled=True)
    grad_down = jnp.einsum("tf,td->fd", active, cot_full, preferred_element_type=jnp.float32)
    grad_active = jnp.einsum("td,fd->tf", cot_full, full_down, preferred_element_type=jnp.float32)
    grad_gate = grad_active * upper * sigma * (1.0 + gate * (1.0 - sigma))
    grad_up = grad_active * gate * sigma
    grad_gu = jnp.stack([grad_gate, grad_up], 1).astype(jnp.bfloat16)
    grad_ffin = jnp.einsum("td,tkf->dkf", hidden, grad_gu, preferred_element_type=jnp.float32)
    grad_hidden = lax.psum_scatter(
        jnp.einsum("tkf,dkf->td", grad_gu, full_ffin, preferred_element_type=jnp.float32),
        "tensor",
        scatter_dimension=0,
        tiled=True,
    )
    grad_gain_second = jnp.sum(grad_hidden * unit_second, 0)
    grad_middle = cotangent.astype(jnp.float32) + norm_back(
        grad_hidden, unit_second, inv_second, gain_second
    )
    grad_mixed = lax.all_gather(grad_middle.astype(jnp.bfloat16), "tensor", axis=0, tiled=True)
    grad_attnout = jnp.einsum(
        "tgc,td->gcd", attended_low, grad_mixed, preferred_element_type=jnp.float32
    )
    grad_att = jnp.einsum(
        "td,gcd->tgc", grad_mixed, full_attnout, preferred_element_type=jnp.float32
    ).astype(jnp.bfloat16)
    grad_q, grad_k, grad_v = attend_backward(
        queries,
        keys,
        vals,
        segments,
        log_norm,
        grad_att.reshape(n_rows, groups, QPK, ADIM),
        q_len,
        scaling,
    )
    grad_q = rotate(grad_q, places, -1.0).reshape(n_rows, groups, QPK * ADIM)
    grad_k = rotate(grad_k, places, -1.0)
    grad_qkv = jnp.concatenate([grad_q, grad_k, grad_v], -1).astype(jnp.bfloat16)
    grad_attn = jnp.einsum("td,tgc->dgc", normed, grad_qkv, preferred_element_type=jnp.float32)
    grad_normed = jnp.einsum("tgc,dgc->td", grad_qkv, full_attn, preferred_element_type=jnp.float32)
    grad_mixout = jnp.einsum(
        "thc,td->hcd", mamba_low, grad_mixed, preferred_element_type=jnp.float32
    )
    grad_mamba = jnp.einsum(
        "td,hcd->thc", grad_mixed, full_mixout, preferred_element_type=jnp.float32
    ).reshape(n_rows, -1)
    (
        grad_zx,
        grad_step,
        grad_bc,
        grad_conv,
        grad_conv_bias,
        grad_conv_bc,
        grad_conv_bc_bias,
        grad_decay,
        grad_step_bias,
        grad_skip,
        grad_gain_mix,
    ) = mamba_pull(grad_mamba)
    grad_zx_low = grad_zx.astype(jnp.bfloat16)
    grad_step_low = grad_step.astype(jnp.bfloat16)
    grad_mix = jnp.einsum("td,thc->dhc", normed, grad_zx_low, preferred_element_type=jnp.float32)
    grad_stepw = jnp.einsum("td,th->dh", normed, grad_step_low, preferred_element_type=jnp.float32)
    normed_wide = normed.astype(jnp.float32)
    grad_statew = jnp.einsum("td,tn->dn", normed_wide, grad_bc, precision=HIGH)
    grad_normed = grad_normed + jnp.einsum(
        "thc,dhc->td", grad_zx_low, full_mix, preferred_element_type=jnp.float32
    )
    grad_normed = grad_normed + jnp.einsum(
        "th,dh->td", grad_step_low, full_step, preferred_element_type=jnp.float32
    )
    grad_normed = grad_normed + jnp.einsum(
        "tn,dn->td", grad_bc, full_state.astype(jnp.float32), precision=HIGH
    )
    grad_normed_loc = lax.psum_scatter(
        grad_normed.astype(jnp.bfloat16), "tensor", scatter_dimension=0, tiled=True
    ).astype(jnp.float32)
    grad_gain_first = jnp.sum(grad_normed_loc * unit_first, 0)
    inputs_grad = grad_middle + norm_back(grad_normed_loc, unit_first, inv_first, gain_first)
    summed = (
        lax.psum_scatter(grad_mix, "dp", scatter_dimension=0, tiled=True),
        lax.psum_scatter(grad_stepw, "dp", scatter_dimension=0, tiled=True),
        lax.psum_scatter(grad_attn, "dp", scatter_dimension=0, tiled=True),
        lax.psum_scatter(grad_mixout, "dp", scatter_dimension=2, tiled=True),
        lax.psum_scatter(grad_attnout, "dp", scatter_dimension=2, tiled=True),
        lax.psum_scatter(grad_ffin, "dp", scatter_dimension=0, tiled=True),
        lax.psum_scatter(grad_down, "dp", scatter_dimension=1, tiled=True),
    )
    small_sums = (
        lax.psum_scatter(grad_gain_first, ("dp", "tensor"), scatter_dimension=0, tiled=True),
        lax.psum_scatter(grad_gain_second, ("dp", "tensor"), scatter_dimension=0, tiled=True),
        lax.psum_scatter(grad_statew, ("dp", "tensor"), scatter_dimension=0, tiled=True),
        lax.psum_scatter(widen(grad_conv, 1), ("dp", "tensor"), scatter_dimension=1, tiled=True),
        lax.psum_scatter(
            widen(grad_conv_bias, 0), ("dp", "tensor"), scatter_dimension=0, tiled=True
        ),
        lax.psum_scatter(
            widen(grad_gain_mix, 0), ("dp", "tensor"), scatter_dimension=0, tiled=True
        ),
        lax.psum_scatter(grad_conv_bc, ("dp", "tensor"), scatter_dimension=1, tiled=True),
        lax.psum_scatter(grad_conv_bc_bias, ("dp", "tensor"), scatter_dimension=0, tiled=True),
    )
    head_sums = lax.psum((grad_decay, grad_step_bias, grad_skip), "dp")
    return (
        output,
        inputs_grad,
        small_sums[0],
        summed[0],
        summed[1],
        small_sums[2],
        small_sums[3],
        small_sums[4],
        small_sums[6],
        small_sums[7],
        head_sums[0],
        head_sums[1],
        head_sums[2],
        small_sums[5],
        summed[2],
        summed[3],
        summed[4],
        small_sums[1],
        summed[5],
        summed[6],
    )


def solution(mesh):
    return jax.shard_map(
        per_device,
        mesh=mesh,
        in_specs=(
            P(("dp", "tensor"), None),
            P("dp"),
            P(("dp", "tensor"), None),
            P(("dp", "tensor")),
            P("dp", "tensor", None),
            P("dp", "tensor"),
            P(("dp", "tensor"), None),
            P(None, ("dp", "tensor")),
            P(("dp", "tensor")),
            P(None, ("dp", "tensor")),
            P(("dp", "tensor")),
            P("tensor"),
            P("tensor"),
            P("tensor"),
            P(("dp", "tensor")),
            P("dp", "tensor", None),
            P("tensor", None, "dp"),
            P("tensor", None, "dp"),
            P(("dp", "tensor")),
            P("dp", None, "tensor"),
            P("tensor", "dp"),
        ),
        out_specs=(
            P(("dp", "tensor"), None),
            P(("dp", "tensor"), None),
            P(("dp", "tensor")),
            P("dp", "tensor", None),
            P("dp", "tensor"),
            P(("dp", "tensor"), None),
            P(None, ("dp", "tensor")),
            P(("dp", "tensor")),
            P(None, ("dp", "tensor")),
            P(("dp", "tensor")),
            P("tensor"),
            P("tensor"),
            P("tensor"),
            P(("dp", "tensor")),
            P("dp", "tensor", None),
            P("tensor", None, "dp"),
            P("tensor", None, "dp"),
            P(("dp", "tensor")),
            P("dp", None, "tensor"),
            P("tensor", "dp"),
        ),
        check_vma=False,
    )
```

profile of v0, /device:TPU:0, one launch (start us, length us, event | category | flops | bytes accessed | tf_op | source)
XLA Modules:
  0.0 1973.9 jit_solution(8028061360457775478)
XLA Ops:
  11.6 42.2 %all-reduce.39 = (bf16[1024]{0:T(1024)(128)(2,1)S(1)}, bf16[256]{0:T(256)(128)(2,1)S(1)}, bf16[1536]{0:T(1024)(128)(2,1)S(1)}, bf16[1536]{0:T(1024)(128)(2,1)S(1)}, bf16[1024]{0:T(1024)(128)(2,1)}) all-reduce(bf16[1024]{0:T(1024)(128)(2,1)S(1)} %dynamic-update-slice.1, ...), channel_id=1, replica_groups=mesh['dp'=16,'tensor'=2] {'dp','tensor'}, use_global_device_ids=true, to_apply=%add.26 | all-reduce | flops 5376 | bytes 21504
  61.5 40.2 %all-gather.2 = bf16[16,64,12]{1,2,0:T(8,128)(2,1)S(1)} all-gather(bf16[1,64,12]{1,2,0:T(8,128)(2,1)S(1)} %bitcast.635), channel_id=1, replica_groups=mesh['dp'=16,'tensor'=2] {'dp'}, dimensions={0}, use_global_device_ids=true | all-gather | bytes 26112 | tf_op jit(solution)/shard_map/all_gather | solution.py:236
  102.4 36.6 %all-gather = bf16[32,48,4]{1,2,0:T(4,128)(2,1)S(1)} all-gather(bf16[1,48,4]{1,2,0:T(4,128)(2,1)S(1)} %bitcast.636), channel_id=1, replica_groups=mesh['dp'=16,'tensor'=2] {'dp','tensor'}, dimensions={0}, use_global_device_ids=true | all-gather | bytes 12672 | tf_op jit(solution)/shard_map/all_gather | solution.py:247
  140.4 42.8 %all_gather.71 = bf16[1024,256]{1,0:T(8,128)(2,1)} all-gather(bf16[32,256]{1,0:T(8,128)(2,1)S(1)} %copy-done.148), channel_id=1, replica_groups=mesh['dp'=16,'tensor'=2] {'dp','tensor'}, dimensions={0}, use_global_device_ids=true | all-gather | bytes 540672 | tf_op jit(solution)/shard_map/all_gather | solution.py:246
  183.9 36.8 %all-gather.1 = bf16[32,8,4]{1,2,0:T(4,128)(2,1)S(1)} all-gather(bf16[1,8,4]{1,2,0:T(4,128)(2,1)S(1)} %bitcast.637), channel_id=1, replica_groups=mesh['dp'=16,'tensor'=2] {'dp','tensor'}, dimensions={0}, use_global_device_ids=true | all-gather | bytes 2112 | tf_op jit(solution)/shard_map/all_gather | solution.py:250
  222.5 42.2 %all_gather.75 = bf16[1024,1,384]{2,0,1:T(8,128)(2,1)S(1)} all-gather(bf16[64,1,384]{2,0,1:T(8,128)(2,1)S(1)} %copy-done.126), channel_id=1, replica_groups=mesh['dp'=16,'tensor'=2] {'dp'}, dimensions={0}, use_global_device_ids=true | all-gather | bytes 835584 | tf_op jit(solution)/shard_map/all_gather | solution.py:237
  265.3 41.0 %all_gather.76 = bf16[1,256,1024]{1,2,0:T(8,128)(2,1)} all-gather(bf16[1,256,64]{1,2,0:T(8,128)(2,1)S(1)} %copy-done.139), channel_id=1, replica_groups=mesh['dp'=16,'tensor'=2] {'dp'}, dimensions={2}, use_global_device_ids=true | all-gather | bytes 557056 | tf_op jit(solution)/shard_map/all_gather | solution.py:239
  324.3 18.2 while.61
  329.8 3.7 fusion.304
  338.8 3.7 fusion.304
  355.4 5.7 copy.319
  361.2 5.5 fusion.134
  369.4 4.6 fusion.96
  377.3 6.3 fusion.105
  384.9 9.7 while.62
  394.7 4.5 fusion.225
  400.9 15.0 fusion.94
  421.4 4.2 bitcast_add_fusion.3
  427.4 8.1 reduce-scatter.20.cloned.1.call-done
  440.6 75.8 %all-gather.20.cloned.1.call-done = bf16[1024,2,1024]{2,0,1:T(8,128)(2,1)} async-done(((bf16[64,2,1024]{2,0,1:T(8,128)(2,1)}), bf16[1024,2,1024]{2,0,1:T(8,128)(2,1)}) %all-gather.20.cloned.1.call-update) | async-done | bytes 4194320 | tf_op jit(solution)/shard_map/all_gather | solution.py:240
  516.4 11.2 all-gather.18.cloned.1.call-done
  527.6 10.9 fusion.130
  541.0 65.1 %all-gather.22.cloned.1.call-done = bf16[1024,1024]{0,1:T(8,128)(2,1)} async-done(((bf16[1024,64]{0,1:T(8,128)(2,1)}), bf16[1024,1024]{0,1:T(8,128)(2,1)}) %all-gather.22.cloned.1.call-update) | async-done | bytes 2097168 | tf_op jit(solution)/shard_map/all_gather | solution.py:241
  606.1 9.9 fusion.137
  617.9 6.2 fusion.118
  624.2 10.8 reduce-scatter.24.cloned.1.call-done
  640.1 11.5 all-gather.26.cloned.1.call-done
  651.6 5.9 multiply_reduce_fusion.2
  657.5 6.4 multiply_reduce_fusion.3
  665.6 4.1 fusion.102
  669.7 21.2 %fusion.71 = (f32[4,256,12]{1,2,0:T(8,128)}, f32[4,256,12]{1,2,0:T(8,128)}, f32[4,256,12]{1,2,0:T(8,128)}, f32[4,256,256]{2,1,0:T(8,128)}) fusion(f32[4,256,12]{1,2,0:T(8,128)S(1)} %copy-done.122, f32[4,256,12]{1,2,0:T(8,128)S(1)} %bitcast.605, f32[4,256,256]{2,1,0:T(8,128)S(1)} %copy-done.78, pred[4,256,256]{2,1,0:T(8,128)(4,1)S(1)} %copy-done.97, ...), kind=kOutput, calls=%fused_computation.89 | convolution fusion | flops 2456514560 | bytes 8896512 | tf_op jit(solution)/shard_map/transpose(jvp(ctsh,cshp->cthp))/dot_general | solution.py:68
  692.2 11.4 while.64
  703.6 4.5 fusion.226
  711.4 12.1 fusion.93
  723.6 5.9 fusion.151
  731.5 58.7 %while.63 = (s32[]{:T(128)}, f32[1024,1,64]{0,2,1:T(8,128)S(1)}, f32[1024,1,64]{0,2,1:T(8,128)}, f32[2,512,1,4,64]{1,0,4,3,2:T(2,128)}, bf16[2,512,1,4,64]{1,4,3...) while((s32[]{:T(128)}, f32[1024,1,64]{0,2,1:T(8,128)S(1)}, ...), condition=%wide.region_19.20_spmd.clone, body=%wide.region_17.19_spmd.clone.sunk | while | flops 1375664128 | bytes 120529128 | solution.py:192
  742.1 10.3 dynamic_update_slice.72
  755.5 5.4 fusion.319
  771.2 10.3 dynamic_update_slice.72
  784.6 5.5 fusion.319
  799.4 10.1 reduce-window.29
  816.8 5.0 multiply_reduce_fusion.6
  837.5 3.6 copy.348
  842.5 6.8 fusion.148
  870.7 4.0 fusion.86
  875.0 6.1 convolution_convert_fusion
  881.1 5.1 fusion.125
  886.3 7.9 copy.383
  894.2 7.3 reshape.1075
  903.1 9.2 fusion.107
  913.9 5.9 fusion.228
  925.3 7.3 fusion.132
  934.5 42.5 %all-reduce.38 = (f32[12]{0:T(128)}, f32[12]{0:T(128)}, f32[12]{0:T(128)}) all-reduce(f32[12]{0:T(128)S(1)} %exponential_multiply_fusion.2, f32[12]{0:T(128)S(1)} %get-tuple-element.786, f32[12]{0:T(128)S(1)} %copy-done.174), channel_id=1, replica_groups=mesh['dp'=16,'tensor'=2] {'dp'}, use_global_device_ids=true, to_apply=%region_54.55 | all-reduce | flops 36 | bytes 288 | tf_op jit(solution)/shard_map/psum | solution.py:478
  979.0 18.8 reduce-scatter.38.cloned.1.call-done
  999.3 112.8 %all-reduce.42.cloned.1.call-done = f32[1,256,1024]{1,0,2:T(1,128)} async-done(((f32[1,256,1024]{1,0,2:T(1,128)}), f32[1,256,1024]{1,0,2:T(1,128)}) %all-reduce.42.cloned.1.call-update) | async-done | bytes 1048592
  1113.6 127.5 %reduce-scatter.32.cloned.1.call-done = f32[64,1,384]{2,0,1:T(8,128)} async-done(((f32[1024,1,384]{2,0,1:T(8,128)}), f32[64,1,384]{2,0,1:T(8,128)}) %reduce-scatter.32.cloned.1.call-update) | async-done | bytes 98320 | tf_op jit(solution)/shard_map/reduce_scatter | solution.py:458
  1242.7 9.2 reduce-scatter.26.cloned.1.call-done
  1254.0 41.1 %all-reduce.37 = (f32[1024]{0:T(1024)S(1)}, f32[1536]{0:T(1024)S(1)}, f32[4,256]{1,0:T(4,128)S(1)}, f32[256]{0:T(256)S(1)}, f32[1536]{0:T(1024)S(1)}, /*index=5*/f32[1024]{0:T(1024)S(1)}) all-reduce(f32[1024]{0:T(1024)S(1)} %get-tuple-element.691, ...), channel_id=6, replica_groups=mesh['dp'=16,'tensor'=2] {'dp','tensor'}, use_global_device_ids=true, to_apply=%region_35.36.clone | all-reduce | flops 6400 | bytes 51200
  1298.7 4.3 fusion.120
  1303.0 99.2 %reduce-scatter.42.cloned.1.call-done = f32[64,768]{1,0:T(8,128)} async-done(((f32[1024,768]{1,0:T(8,128)}), f32[64,768]{1,0:T(8,128)}) %reduce-scatter.42.cloned.1.call-update) | async-done | bytes 196624
  1404.3 177.3 %reduce-scatter.34.cloned.1.call-done = f32[64,2,1024]{2,0,1:T(8,128)} async-done(((f32[1024,2,1024]{2,0,1:T(8,128)}), f32[64,2,1024]{2,0,1:T(8,128)}) %reduce-scatter.34.cloned.1.call-update) | async-done | bytes 524304 | tf_op jit(solution)/shard_map/reduce_scatter | solution.py:461
  1583.8 98.3 %reduce-scatter.36.cloned.1.call-done = f32[1024,64]{0,1:T(8,128)} async-done(((f32[1024,1024]{0,1:T(8,128)}), f32[1024,64]{0,1:T(8,128)}) %reduce-scatter.36.cloned.1.call-update) | async-done | bytes 262160 | tf_op jit(solution)/shard_map/reduce_scatter | solution.py:462
  1682.1 137.2 %reduce-scatter.30.cloned.1.call-done = f32[32,256]{1,0:T(8,128)} async-done(((f32[1024,256]{1,0:T(8,128)}), f32[32,256]{1,0:T(8,128)}) %reduce-scatter.30.cloned.1.call-update) | async-done | bytes 32784 | tf_op jit(solution)/shard_map/reduce_scatter | solution.py:467
  1819.3 147.6 %reduce-scatter.28.cloned.1.call-done = f32[64,12,128]{2,0,1:T(8,128)} async-done(((f32[1024,12,128]{2,0,1:T(8,128)}), f32[64,12,128]{2,0,1:T(8,128)}) %reduce-scatter.28.cloned.1.call-update) | async-done | bytes 393232 | tf_op jit(solution)/shard_map/reduce_scatter | solution.py:456
  (672 shorter events, 225.5 us)
Async XLA Ops:
  7.2 50.8 %copy-start.105 = (bf16[12,64,64]{2,1,0:T(8,128)(2,1)S(1)}, bf16[12,64,64]{2,1,0:T(8,128)(2,1)}, u32[]{:S(2)}) copy-start(bf16[12,64,64]{2,1,0:T(8,128)(2,1)} %param.45) | copy-start | bytes 294916
  7.2 52.5 %copy-start.80 = (s32[1024]{0:T(1024)S(1)}, s32[1024]{0:T(1024)}, u32[]{:S(2)}) copy-start(s32[1024]{0:T(1024)} %param.30) | copy-start | bytes 12292
  7.2 54.3 %copy-start.166 = (bf16[64,12]{0,1:T(8,128)(2,1)S(1)}, bf16[64,12]{0,1:T(8,128)(2,1)}, u32[]{:S(2)}) copy-start(bf16[64,12]{0,1:T(8,128)(2,1)} %param.34) | copy-start | bytes 4612
  7.2 94.6 %copy-start.179 = (f32[12]{0:T(128)S(1)}, f32[12]{0:T(128)}, u32[]{:S(2)}) copy-start(f32[12]{0:T(128)} %param.40) | copy-start | bytes 148
  7.2 95.1 %copy-start.172 = (bf16[4,48]{1,0:T(4,128)(2,1)S(1)}, bf16[4,48]{1,0:T(4,128)(2,1)}, u32[]{:S(2)}) copy-start(bf16[4,48]{1,0:T(4,128)(2,1)} %param.36) | copy-start | bytes 1156
  7.2 133.2 %copy-start.148 = (bf16[32,256]{1,0:T(8,128)(2,1)S(1)}, bf16[32,256]{1,0:T(8,128)(2,1)}, u32[]{:S(2)}) copy-start(bf16[32,256]{1,0:T(8,128)(2,1)} %param.35) | copy-start | bytes 49156
  7.3 302.5 %all-gather.12.cloned.1.call-start = ((), (), s32[]{:S(2)}) async-start(), calls=%async_computation.12 | async-start | bytes 3145728 | tf_op jit(solution)/shard_map/all_gather | solution.py:280
  53.8 130.1 %copy-start.173 = (bf16[4,8]{1,0:T(4,128)(2,1)S(1)}, bf16[4,8]{1,0:T(4,128)(2,1)}, u32[]{:S(2)}) copy-start(bf16[4,8]{1,0:T(4,128)(2,1)} %param.38) | copy-start | bytes 196
  55.3 167.2 %copy-start.126 = (bf16[64,1,384]{2,0,1:T(8,128)(2,1)S(1)}, bf16[64,1,384]{2,0,1:T(8,128)(2,1)}, u32[]{:S(2)}) copy-start(bf16[64,1,384]{2,0,1:T(8,128)(2,1)} %param.44) | copy-start | bytes 147460
  55.3 83.8 %copy-start.140 = (f32[512]{0:T(512)}, f32[512]{0:T(512)S(1)}, u32[]{:S(2)}) copy-start(f32[512]{0:T(512)S(1)} %add_rsqrt_fusion.1) | copy-start | bytes 6148
  55.3 210.0 %copy-start.139 = (bf16[1,256,64]{1,2,0:T(8,128)(2,1)S(1)}, bf16[1,256,64]{1,2,0:T(8,128)(2,1)}, u32[]{:S(2)}) copy-start(bf16[1,256,64]{1,2,0:T(8,128)(2,1)} %param.46) | copy-start | bytes 98308
  57.9 297.5 %all-gather.16.cloned.1.call-start = ((), (), s32[]{:S(2)}) async-start(), calls=%async_computation.14 | async-start | bytes 4456448 | tf_op jit(solution)/shard_map/all_gather | solution.py:238
  58.9 302.2 %all-gather.14.cloned.1.call-start = ((), (), s32[]{:S(2)}) async-start(), calls=%async_computation.13 | async-start | bytes 3342336 | tf_op jit(solution)/shard_map/all_gather | solution.py:235
  59.7 375.8 %reduce-scatter.20.cloned.1.call-start = ((), (), s32[]{:S(2)}) async-start(), calls=%async_computation.15 | async-start | bytes 6291456 | tf_op jit(solution)/shard_map/reduce_scatter | solution.py:351
  60.2 309.1 %copy-start.99 = (f32[1024]{0:T(1024)}, f32[1024]{0:T(1024)S(1)}, u32[]{:S(2)}) copy-start(f32[1024]{0:T(1024)S(1)} %get-tuple-element.851) | copy-start | bytes 12292
  60.2 309.1 %copy-start.101 = (f32[1024]{0:T(1024)}, f32[1024]{0:T(1024)S(1)}, u32[]{:S(2)}) copy-start(f32[1024]{0:T(1024)S(1)} %get-tuple-element.852) | copy-start | bytes 12292
  60.2 309.1 %copy-start.103 = (f32[1024]{0:T(1024)}, f32[1024]{0:T(1024)S(1)}, u32[]{:S(2)}) copy-start(f32[1024]{0:T(1024)S(1)} %get-tuple-element.853) | copy-start | bytes 12292
  60.3 249.4 %copy-start.162 = (f32[32]{0:T(128)}, f32[32]{0:T(128)S(1)}, u32[]{:S(2)}) copy-start(f32[32]{0:T(128)S(1)} %multiply_power_fusion) | copy-start | bytes 388
  101.8 213.0 %copy-start.90 = (bf16[1024,12]{0,1:T(8,128)(2,1)}, bf16[1024,12]{0,1:T(8,128)(2,1)S(1)}, u32[]{:S(2)}) copy-start(bf16[1024,12]{0,1:T(8,128)(2,1)S(1)} %reshape.1037) | copy-start | bytes 73732
  264.7 48.9 %copy-start.55 = (bf16[1024,1,384]{2,0,1:T(8,128)(2,1)}, bf16[1024,1,384]{2,0,1:T(8,128)(2,1)S(1)}, u32[]{:S(2)}) copy-start(bf16[1024,1,384]{2,0,1:T(8,128)(2,1)S(1)} %all_gather.75) | copy-start | bytes 2359300
  265.3 48.3 %copy-start.117 = (f32[1024]{0:T(1024)}, f32[1024]{0:T(1024)S(1)}, u32[]{:S(2)}) copy-start(f32[1024]{0:T(1024)S(1)} %fusion.199) | copy-start | bytes 12292
  319.2 26.1 %copy-start.70 = (f32[4,12,256]{2,1,0:T(8,128)}, f32[4,12,256]{2,1,0:T(8,128)S(1)}, u32[]{:S(2)}) copy-start(f32[4,12,256]{2,1,0:T(8,128)S(1)} %reshape.1066) | copy-start | bytes 147460
  319.2 26.0 %copy-start.81 = (f32[4,256,12]{1,0,2:T(4,128)}, f32[4,256,12]{1,0,2:T(4,128)S(1)}, u32[]{:S(2)}) copy-start(f32[4,256,12]{1,0,2:T(4,128)S(1)} %mul.993) | copy-start | bytes 147460
  324.3 21.0 %copy-start.119 = (f32[4,256]{1,0:T(4,128)S(1)}, f32[4,256]{1,0:T(4,128)}, u32[]{:S(2)}) copy-start(f32[4,256]{1,0:T(4,128)} %get-tuple-element.844) | copy-start | bytes 12292
  324.3 21.0 %copy-start.135 = (f32[4,256]{1,0:T(4,128)S(1)}, f32[4,256]{1,0:T(4,128)}, u32[]{:S(2)}) copy-start(f32[4,256]{1,0:T(4,128)} %get-tuple-element.843) | copy-start | bytes 12292
  373.9 42.5 %copy-start.6 = (f32[1024,768]{0,1:T(8,128)}, f32[1024,768]{0,1:T(8,128)S(1)}, u32[]{:S(2)}) copy-start(f32[1024,768]{0,1:T(8,128)S(1)} %get-tuple-element.794) | copy-start | bytes 9437188
  394.7 21.8 %slice-start = ((s8[6291456]{0:T(1024)(128)(4,1)}), s8[4194304]{0:T(1024)(128)(4,1)S(1)}, s32[]{:S(2)}) async-start(s8[6291456]{0:T(1024)(128)(4,1)} %bitcast.580), calls=%async_computation.33 | async-start | bytes 8388608
  418.5 233.0 %copy-start.144 = (f32[1024]{0:T(1024)}, f32[1024]{0:T(1024)S(1)}, u32[]{:S(2)}) copy-start(f32[1024]{0:T(1024)S(1)} %fusion.205) | copy-start | bytes 12292
  425.6 90.8 %all-gather.20.cloned.1.call-start = ((), (), s32[]{:S(2)}) async-start(), calls=%async_computation.17 | async-start | bytes 4456448 | tf_op jit(solution)/shard_map/all_gather | solution.py:240
  427.3 100.3 %all-gather.18.cloned.1.call-start = ((), (), s32[]{:S(2)}) async-start(), calls=%async_computation.16 | async-start | bytes 3145728 | tf_op jit(solution)/shard_map/all_gather | solution.py:355
  427.4 210.5 %copy-start.108 = (f32[1024]{0:T(1024)}, f32[1024]{0:T(1024)S(1)}, u32[]{:S(2)}) copy-start(f32[1024]{0:T(1024)S(1)} %convert_element_type.171) | copy-start | bytes 12292
  437.4 200.5 %copy-start.4 = (f32[512,1024]{1,0:T(8,128)}, f32[512,1024]{1,0:T(8,128)S(1)}, u32[]{:S(2)}) copy-start(f32[512,1024]{1,0:T(8,128)S(1)} %get-tuple-element.791) | copy-start | bytes 6291460
  437.4 200.5 %copy-start.124 = (f32[512]{0:T(512)}, f32[512]{0:T(512)S(1)}, u32[]{:S(2)}) copy-start(f32[512]{0:T(512)S(1)} %add_rsqrt_fusion) | copy-start | bytes 6148
  438.8 102.2 %all-gather.24.cloned.1.call-start = ((), (), s32[]{:S(2)}) async-start(), calls=%async_computation.20 | async-start | bytes 3145728 | tf_op jit(solution)/shard_map/all_gather | solution.py:377
  439.6 166.5 %all-gather.22.cloned.1.call-start = ((), (), s32[]{:S(2)}) async-start(), calls=%async_computation.18 | async-start | bytes 2228224 | tf_op jit(solution)/shard_map/all_gather | solution.py:241
  440.3 194.7 %reduce-scatter.24.cloned.1.call-start = ((), (), s32[]{:S(2)}) async-start(), calls=%async_computation.21 | async-start | bytes 6291456 | tf_op jit(solution)/shard_map/reduce_scatter | solution.py:384
  624.1 27.4 %all-gather.26.cloned.1.call-start = ((), (), s32[]{:S(2)}) async-start(), calls=%async_computation.22 | async-start | bytes 3145728 | tf_op jit(solution)/shard_map/all_gather | solution.py:394
  639.6 338.1 %reduce-scatter.40.cloned.1.call-start = ((), (), s32[]{:S(2)}) async-start(), calls=%async_computation.30 | async-start | bytes 811008
  663.9 59.6 %copy-start.2 = (f32[1024,12,64]{0,2,1:T(8,128)}, f32[1024,12,64]{0,2,1:T(8,128)S(1)}, u32[]{:S(2)}) copy-start(f32[1024,12,64]{0,2,1:T(8,128)S(1)} %get-tuple-element.785) | copy-start | bytes 9437188
  731.4 62.0 %copy-start.74 = (f32[4,12,256]{2,1,0:T(8,128)S(1)}, f32[4,12,256]{2,1,0:T(8,128)}, u32[]{:S(2)}) copy-start(f32[4,12,256]{2,1,0:T(8,128)} %copy-done.70) | copy-start | bytes 147460
  731.4 62.0 %copy-start.82 = (f32[4,256,12]{1,0,2:T(4,128)S(1)}, f32[4,256,12]{1,0,2:T(4,128)}, u32[]{:S(2)}) copy-start(f32[4,256,12]{1,0,2:T(4,128)} %copy-done.81) | copy-start | bytes 147460
  731.4 62.0 %copy-start.114 = (f32[4,12]{1,0:T(4,128)S(1)}, f32[4,12]{1,0:T(4,128)}, u32[]{:S(2)}) copy-start(f32[4,12]{1,0:T(4,128)} %copy-done.113) | copy-start | bytes 580
  731.4 62.0 %copy-start.120 = (f32[4,256]{1,0:T(4,128)S(1)}, f32[4,256]{1,0:T(4,128)}, u32[]{:S(2)}) copy-start(f32[4,256]{1,0:T(4,128)} %get-tuple-element.844) | copy-start | bytes 12292
  731.4 65.3 %copy-start.136 = (f32[4,256]{1,0:T(4,128)S(1)}, f32[4,256]{1,0:T(4,128)}, u32[]{:S(2)}) copy-start(f32[4,256]{1,0:T(4,128)} %get-tuple-element.843) | copy-start | bytes 12292
  790.1 21.9 %copy-start.57 = (f32[4,12,8,8,256]{4,3,2,1,0:T(8,128)S(1)}, f32[4,12,8,8,256]{4,3,2,1,0:T(8,128)}, u32[]{:S(2)}) copy-start(f32[4,12,8,8,256]{4,3,2,1,0:T(8,128)} %fusion.93) | copy-start | bytes 9437188
  823.1 174.7 %reduce-scatter.38.cloned.1.call-start = ((), (), s32[]{:S(2)}) async-start(), calls=%async_computation.29 | async-start | bytes 557056
  832.9 279.2 %all-reduce.42.cloned.1.call-start = ((), (), s32[]{:S(2)}) async-start(), calls=%async_computation.32 | async-start | bytes 2097152
  841.2 399.9 %reduce-scatter.32.cloned.1.call-start = ((), (), s32[]{:S(2)}) async-start(), calls=%async_computation.26 | async-start | bytes 1671168 | tf_op jit(solution)/shard_map/reduce_scatter | solution.py:458
  853.8 398.1 %reduce-scatter.26.cloned.1.call-start = ((), (), s32[]{:S(2)}) async-start(), calls=%async_computation.23 | async-start | bytes 3145728 | tf_op jit(solution)/shard_map/reduce_scatter | solution.py:450
  874.7 423.9 %reduce-scatter.22.cloned.1.call-start = ((), (), s32[]{:S(2)}) async-start(), calls=%async_computation.19 | async-start | bytes 3145728 | tf_op jit(solution)/shard_map/reduce_scatter | solution.py:364
  881.1 521.2 %reduce-scatter.42.cloned.1.call-start = ((), (), s32[]{:S(2)}) async-start(), calls=%async_computation.31 | async-start | bytes 3342336
  901.5 680.1 %reduce-scatter.34.cloned.1.call-start = ((), (), s32[]{:S(2)}) async-start(), calls=%async_computation.27 | async-start | bytes 8912896 | tf_op jit(solution)/shard_map/reduce_scatter | solution.py:461
  912.3 769.8 %reduce-scatter.36.cloned.1.call-start = ((), (), s32[]{:S(2)}) async-start(), calls=%async_computation.28 | async-start | bytes 4456448 | tf_op jit(solution)/shard_map/reduce_scatter | solution.py:462
  919.8 899.4 %reduce-scatter.30.cloned.1.call-start = ((), (), s32[]{:S(2)}) async-start(), calls=%async_computation.25 | async-start | bytes 1081344 | tf_op jit(solution)/shard_map/reduce_scatter | solution.py:467
  925.0 1041.8 %reduce-scatter.28.cloned.1.call-start = ((), (), s32[]{:S(2)}) async-start(), calls=%async_computation.24 | async-start | bytes 6684672 | tf_op jit(solution)/shard_map/reduce_scatter | solution.py:456
  932.6 44.4 %copy-start.157 = (f32[12,64]{1,0:T(8,128)S(1)}, f32[12,64]{1,0:T(8,128)}, u32[]{:S(2)}) copy-start(f32[12,64]{1,0:T(8,128)} %get-tuple-element.682) | copy-start | bytes 9220
  932.6 319.3 %copy-start.18 = (bf16[512,1024]{1,0:T(8,128)(2,1)S(1)}, bf16[512,1024]{1,0:T(8,128)(2,1)}, u32[]{:S(2)}) copy-start(bf16[512,1024]{1,0:T(8,128)(2,1)} %param.29) | copy-start | bytes 3145732
  932.6 319.3 %copy-start.116 = (f32[1024]{0:T(1024)S(1)}, f32[1024]{0:T(1024)}, u32[]{:S(2)}) copy-start(f32[1024]{0:T(1024)} %copy-done.115) | copy-start | bytes 12292
  932.6 319.3 %copy-start.141 = (f32[512]{0:T(512)S(1)}, f32[512]{0:T(512)}, u32[]{:S(2)}) copy-start(f32[512]{0:T(512)} %copy-done.140) | copy-start | bytes 6148
  932.7 321.3 %copy-start.147 = (f32[1024]{0:T(1024)S(1)}, f32[1024]{0:T(1024)}, u32[]{:S(2)}) copy-start(f32[1024]{0:T(1024)} %get-tuple-element.687) | copy-start | bytes 12292
  932.7 366.0 %copy-start.5 = (f32[512,1024]{1,0:T(8,128)S(1)}, f32[512,1024]{1,0:T(8,128)}, u32[]{:S(2)}) copy-start(f32[512,1024]{1,0:T(8,128)} %copy-done.4) | copy-start | bytes 6291460
  932.7 366.0 %copy-start.109 = (f32[1024]{0:T(1024)S(1)}, f32[1024]{0:T(1024)}, u32[]{:S(2)}) copy-start(f32[1024]{0:T(1024)} %copy-done.108) | copy-start | bytes 12292
  932.7 366.0 %copy-start.125 = (f32[512]{0:T(512)S(1)}, f32[512]{0:T(512)}, u32[]{:S(2)}) copy-start(f32[512]{0:T(512)} %copy-done.124) | copy-start | bytes 6148
  932.7 366.0 %copy-start.143 = (f32[512]{0:T(512)S(1)}, f32[512]{0:T(512)}, u32[]{:S(2)}) copy-start(f32[512]{0:T(512)} %copy-done.142) | copy-start | bytes 6148
  (145 other events, 647.6 us)
Sparse Core Ops, SparseCore 0:
  58.0 10.8 all-gather.11
  72.3 78.9 all-gather.15
  154.0 67.9 all-gather.13
  425.7 9.6 reduce-scatter.19
  439.0 77.3 all-gather.19
  518.4 9.1 all-gather.17
  529.2 11.7 all-gather.23
  544.1 61.8 all-gather.21
  624.2 10.7 reduce-scatter.23
  639.7 11.8 all-gather.25
  823.3 96.6 reduce-scatter.39
  922.1 75.7 reduce-scatter.37
  1004.0 108.0 all-reduce.41
  1117.5 123.5 reduce-scatter.31
  1243.3 8.5 reduce-scatter.25
  1254.0 10.7 reduce-scatter.21
  1270.4 131.7 reduce-scatter.41
  1404.5 177.0 reduce-scatter.33
  1584.6 97.5 reduce-scatter.35
  1684.9 134.3 reduce-scatter.29
  1825.1 141.7 reduce-scatter.27
where the time goes:
time: 1980 us; the launch traced here: 1970 us
  waiting for transfers between devices  1120 us (57%)
  blocking collectives  365 us (18%)
  matrix products  232 us (12%)
  local copies, waits for them, and re-layouts  128 us (6%)
  other arithmetic  113 us (6%)
    unnamed x25, waiting for transfers between devices  233 us
    reduce_scatter x1, waiting for transfers between devices, per_device(): lax.psum_scatter(grad_ffin, 'dp', scatter_dimension=0, tiled=True)  177 us
    reduce_scatter x1, waiting for transfers between devices, per_device(): lax.psum_scatter(grad_mix, 'dp', scatter_dimension=0, tiled=True)  148 us
    reduce_scatter x1, waiting for transfers between devices, per_device(): lax.psum_scatter(grad_statew, ('dp', 'tensor'), scatter_dimension=0, tile...  137 us
    reduce_scatter x1, waiting for transfers between devices, per_device(): lax.psum_scatter(grad_attn, 'dp', scatter_dimension=0, tiled=True)  128 us
    reduce_scatter x1, waiting for transfers between devices, per_device(): lax.psum_scatter(grad_down, 'dp', scatter_dimension=1, tiled=True)  98.3 us
    unnamed x2, blocking collectives  83.3 us
    all_gather x1, waiting for transfers between devices, per_device(): lax.all_gather(ffn_in, 'dp', axis=0, tiled=True)  75.8 us
  transfers between devices with their start and end apart: 21, of which 16 were waited for; matrix products, arithmetic and copies ran while one was open for 10% of the time, Pallas kernels for 0%

commit v1 on v0

v1 whole, which is shorter than its diff:
```python
import jax
import jax.numpy as jnp
from jax import lax
from jax.sharding import PartitionSpec as P

QPK = 4
ADIM = 64
NGH = 12
BLK = 256
QBLK = 512

PREC = lax.Precision.HIGH
EXACT = lax.Precision.HIGHEST
EPS = 1e-05
ROPE_BASE = 100000000000.0
F32 = jnp.float32
BF16 = jnp.bfloat16


def grid_of(size):
    if size == 16:
        return (4, 2, 2)
    factors = []
    while size % 4 == 0:
        factors.append(4)
        size //= 4
    if size > 1 or not factors:
        factors.append(size)
    return tuple(factors)


def coordinates(index, factors):
    coords = []
    for size in reversed(factors):
        coords.append(index % size)
        index = index // size
    return coords[::-1]


def pairs_of(factors, axis, keep, target):
    stride = 1
    for size in factors[axis + 1 :]:
        stride *= size
    total = 1
    for size in factors:
        total *= size
    found = []
    for index in range(total):
        place = coordinates(index, factors)[axis]
        if keep(place):
            found.append((index, index + (target(place) - place) * stride))
    return found


def gather_axis(block, factors, axis, coord):
    size = factors[axis]
    if size == 1:
        return block
    if size == 2:
        other = lax.ppermute(
            block, "dp", pairs_of(factors, axis, lambda c: True, lambda c: 1 - c)
        )
        candidates = [other, block, other]
    else:
        below, above = [], []
        upward, downward = block, block
        for step in range(1, size):
            upward = lax.ppermute(
                upward,
                "dp",
                pairs_of(factors, axis, lambda c: step - 1 <= c < size - 1, lambda c: c + 1),
            )
            downward = lax.ppermute(
                downward,
                "dp",
                pairs_of(factors, axis, lambda c: 1 <= c <= size - step, lambda c: c - 1),
            )
            below.append(upward)
            above.append(downward)
        candidates = below[::-1] + [block] + above
    return lax.dynamic_slice_in_dim(
        jnp.concatenate(candidates, axis), (size - 1 - coord) * block.shape[axis], size, axis
    )


def gather_rows(shard, factors, coords):
    n_axes = len(factors)
    half = shard.shape[0] // 2
    halves = []
    for part, order in ((0, range(1, n_axes)), (1, range(n_axes - 1, 0, -1))):
        block = shard[part * half : (part + 1) * half]
        block = block.reshape((1,) * n_axes + block.shape)
        for axis in (0, *order):
            block = gather_axis(block, factors, axis, coords[axis])
        halves.append(block)
    whole = jnp.concatenate(halves, n_axes)
    return whole.reshape(-1, shard.shape[1])


def reduce_axis(blocks, factors, axis, coord):
    size = factors[axis]
    if size == 1:
        return blocks
    kind = blocks.dtype

    def pick(place):
        return lax.dynamic_slice_in_dim(blocks, jnp.clip(place, 0, size - 1), 1, axis)

    own = pick(coord).astype(F32)
    if size == 2:
        got = lax.ppermute(
            pick(1 - coord), "dp", pairs_of(factors, axis, lambda c: True, lambda c: 1 - c)
        )
        return (own + got.astype(F32)).astype(kind)
    upward, downward = None, None
    for step in range(1, size):
        away = size - step
        send_up, send_down = pick(coord + away), pick(coord - away)
        if upward is not None:
            send_up = (send_up.astype(F32) + upward.astype(F32)).astype(kind)
            send_down = (send_down.astype(F32) + downward.astype(F32)).astype(kind)
        upward = lax.ppermute(
            send_up, "dp", pairs_of(factors, axis, lambda c: c < step, lambda c: c + 1)
        )
        downward = lax.ppermute(
            send_down, "dp", pairs_of(factors, axis, lambda c: c >= away, lambda c: c - 1)
        )
    return (own + upward.astype(F32) + downward.astype(F32)).astype(kind)


def scatter_rows(full, factors, coords):
    n_axes = len(factors)
    total = 1
    for size in factors:
        total *= size
    rows = full.shape[0] // total
    half = rows // 2
    shaped = full.reshape(tuple(factors) + (rows, full.shape[1]))
    halves = []
    for part, order in ((0, range(n_axes - 1, 0, -1)), (1, range(1, n_axes))):
        block = lax.slice_in_dim(shaped, part * half, (part + 1) * half, axis=n_axes)
        for axis in (*order, 0):
            block = reduce_axis(block, factors, axis, coords[axis])
        halves.append(block.reshape(half, full.shape[1]))
    return jnp.concatenate(halves, 0)


def swap(value):
    return lax.ppermute(value, "tensor", [(0, 1), (1, 0)])


def join_tensor(mine, part, axis=0):
    other = swap(mine)
    return lax.dynamic_slice_in_dim(
        jnp.concatenate([other, mine, other], axis),
        (1 - part) * mine.shape[axis],
        2 * mine.shape[axis],
        axis,
    )


def split_tensor(value, part):
    half = value.shape[0] // 2
    give = lax.dynamic_slice_in_dim(value, (1 - part) * half, half, 0).astype(BF16)
    keep = lax.dynamic_slice_in_dim(value, part * half, half, 0).astype(F32)
    return keep + swap(give).astype(F32)


def rotate(values, cosine, sine):
    half_dim = values.shape[-1] // 2
    bshape = (values.shape[0],) + (1,) * (values.ndim - 2) + (half_dim,)
    cosine = cosine.reshape(bshape)
    sine = sine.reshape(bshape)
    first_half = values[..., :half_dim]
    second_half = values[..., half_dim:]
    return jnp.concatenate(
        [first_half * cosine - second_half * sine, second_half * cosine + first_half * sine], -1
    )


def seg_conv(values, taps, shift_bias, same_doc):
    n_rows = values.shape[0]
    n_taps = taps.shape[0]
    padded = jnp.pad(values, ((n_taps - 1, 0), (0, 0)))
    result = shift_bias[None, :] + taps[n_taps - 1][None, :] * values
    for offset in range(n_taps - 1):
        result = (
            result
            + taps[offset][None, :] * padded[offset : offset + n_rows] * same_doc[offset][:, None]
        )
    return result


def ssd_scan(inner, steps, decays, b_state, c_state, segment, block_len):
    n_rows, n_heads, head_dim = inner.shape
    n_blocks = n_rows // block_len
    x_blk = inner.reshape(n_blocks, block_len, n_heads, head_dim).transpose(0, 2, 1, 3)
    dt_blk = steps.reshape(n_blocks, block_len, n_heads).transpose(0, 2, 1)
    within = jnp.arange(block_len, dtype=jnp.int32)
    causal = within[:, None] >= within[None, :]
    cumul = jnp.einsum(
        "ts,csh->cht",
        causal.astype(F32),
        decays.reshape(n_blocks, block_len, n_heads),
        precision=EXACT,
    )
    b_blk = b_state.reshape(n_blocks, block_len, -1)
    c_blk = c_state.reshape(n_blocks, block_len, -1)
    seg_blk = segment.reshape(n_blocks, block_len)
    allowed = (seg_blk[:, :, None] == seg_blk[:, None, :]) & causal[None]
    differ = cumul[:, :, :, None] - cumul[:, :, None, :]
    kernel = jnp.exp(jnp.where(allowed[:, None], differ, -1e30))
    inner_prod = jnp.einsum("ctn,csn->cts", c_blk, b_blk, precision=PREC)
    x_step = x_blk * dt_blk[..., None]
    weights_ts = inner_prod[:, None] * kernel
    y_inner = jnp.einsum("chts,chsp->chtp", weights_ts, x_step, precision=PREC)
    last_seg = seg_blk[:, -1]
    to_end = (
        jnp.exp(cumul[:, :, -1:] - cumul)
        * (seg_blk == last_seg[:, None]).astype(F32)[:, None, :]
    )
    local_state = jnp.einsum(
        "chsp,csn->chpn", x_step * to_end[..., None], b_blk, precision=PREC
    )
    prev_seg = jnp.concatenate([jnp.full((1,), -1, dtype=jnp.int32), last_seg[:-1]])
    carry_keep = jnp.exp(cumul[:, :, -1]) * (last_seg == prev_seg).astype(F32)[:, None]
    state = jnp.zeros(local_state.shape[1:], F32)
    entering = [state]
    for block in range(n_blocks - 1):
        state = state * carry_keep[block][:, None, None] + local_state[block]
        entering.append(state)
    entering = jnp.stack(entering)
    from_start = jnp.exp(cumul) * (seg_blk == prev_seg[:, None]).astype(F32)[:, None, :]
    y_state = jnp.einsum("ctn,chpn->chtp", c_blk, entering, precision=PREC)
    total = y_inner + y_state * from_start[..., None]
    return total.transpose(0, 2, 1, 3).reshape(n_rows, n_heads * head_dim)


def mamba_core(
    gate_z,
    proj_x,
    proj_step,
    proj_bc,
    conv_w,
    conv_b,
    conv_s,
    conv_sb,
    log_decay,
    bias_step,
    gain_skip,
    gain_mix,
    segment,
    same_doc,
):
    n_rows, n_channels = gate_z.shape
    n_heads = proj_step.shape[1]
    head_dim = n_channels // n_heads
    x_conv = jax.nn.silu(seg_conv(proj_x, conv_w, conv_b, same_doc))
    bc_conv = jax.nn.silu(seg_conv(proj_bc, conv_s, conv_sb, same_doc))
    n_state = proj_bc.shape[1] // 2
    steps = jax.nn.softplus(proj_step + bias_step[None, :])
    decays = -steps * jnp.exp(log_decay)[None, :]
    ssm = ssd_scan(
        x_conv.reshape(n_rows, n_heads, head_dim),
        steps,
        decays,
        bc_conv[:, :n_state],
        bc_conv[:, n_state:],
        segment,
        BLK,
    )
    ssm = ssm + jnp.repeat(gain_skip, head_dim)[None, :] * x_conv
    gated = ssm * jax.nn.silu(gate_z)
    width = NGH * head_dim
    normed = []
    for first in range(0, n_channels, width):
        group = gated[:, first : first + width]
        normed.append(group * lax.rsqrt(jnp.mean(group * group, -1, keepdims=True) + EPS))
    return jnp.concatenate(normed, 1) * gain_mix[None, :]


def masked_scores(q_blk, keys, allowed, scaling):
    scores = jnp.einsum("tqd,sd->qts", q_blk, keys, preferred_element_type=F32) * scaling
    return jnp.where(allowed[None], scores, -1e30)


def query_blocks(segment):
    n_rows = segment.shape[0]
    q_len = min(QBLK, n_rows)
    index = jnp.arange(n_rows, dtype=jnp.int32)
    blocks = []
    for start in range(0, n_rows, q_len):
        stop = start + q_len
        allowed = (segment[start:stop, None] == segment[None, :stop]) & (
            index[start:stop, None] >= index[None, :stop]
        )
        blocks.append((start, stop, allowed))
    return blocks


def attend_forward(queries, keys, vals, blocks, scaling):
    outs, norms = [], []
    for start, stop, allowed in blocks:
        scores = masked_scores(queries[start:stop], keys[:stop], allowed, scaling)
        topmost = jnp.max(scores, -1, keepdims=True)
        expo = jnp.exp(scores - topmost)
        total = jnp.sum(expo, -1, keepdims=True)
        probs = (expo / total).astype(BF16)
        outs.append(jnp.einsum("qts,sd->tqd", probs, vals[:stop], preferred_element_type=F32))
        norms.append(topmost + jnp.log(total))
    return jnp.concatenate(outs, 0), norms


def attend_backward(queries, keys, vals, blocks, norms, grad_out, scaling):
    grad_q = []
    grad_keys = jnp.zeros(keys.shape, F32)
    grad_vals = jnp.zeros(vals.shape, F32)
    for (start, stop, allowed), norm in zip(blocks, norms):
        q_blk, dout = queries[start:stop], grad_out[start:stop]
        scores = masked_scores(q_blk, keys[:stop], allowed, scaling)
        probs = jnp.exp(scores - norm)
        dv = jnp.einsum("qts,tqd->sd", probs.astype(BF16), dout, preferred_element_type=F32)
        dprobs = jnp.einsum("tqd,sd->qts", dout, vals[:stop], preferred_element_type=F32)
        dscores = probs * (dprobs - jnp.sum(probs * dprobs, -1, keepdims=True))
        low = dscores.astype(BF16)
        grad_q.append(
            jnp.einsum("qts,sd->tqd", low, keys[:stop], preferred_element_type=F32) * scaling
        )
        dk = jnp.einsum("qts,tqd->sd", low, q_blk, preferred_element_type=F32) * scaling
        tail = ((0, keys.shape[0] - stop), (0, 0))
        grad_keys = grad_keys + jnp.pad(dk, tail)
        grad_vals = grad_vals + jnp.pad(dv, tail)
    return jnp.concatenate(grad_q, 0), grad_keys, grad_vals


def norm_back(grad_normed, unit_rows, inv_scale, gain):
    scaled = grad_normed * gain[None, :]
    return inv_scale * (scaled - unit_rows * jnp.mean(scaled * unit_rows, -1, keepdims=True))


def dot(a, b, dims):
    return lax.dot_general(a, b, (dims, ((), ())), preferred_element_type=F32)


def per_device(
    inputs,
    segments,
    cotangent,
    norm_gain,
    mix_in,
    step_in,
    state_in,
    conv_inner,
    conv_inner_bias,
    conv_state,
    conv_state_bias,
    decay_log,
    step_bias,
    skip_gain,
    mixer_gain,
    attn_in,
    mixer_out,
    attn_out,
    ffn_gain,
    ffn_in,
    ffn_down,
):
    part = lax.axis_index("tensor")
    place = lax.axis_index("dp")
    n_dp = lax.axis_size("dp")
    n_parts = lax.axis_size("tensor")
    factors = grid_of(n_dp)
    coords = coordinates(place, factors)
    rows = mix_in.shape[0]
    n_heads, twice = mix_in.shape[1:]
    head_dim = twice // 2
    inner = n_heads * head_dim
    n_rows = segments.shape[0]
    qkv_cols = attn_in.shape[1] * attn_in.shape[2]
    state_cols = state_in.shape[1]
    hid = ffn_down.shape[0]
    attn_cols = attn_out.shape[0] * attn_out.shape[1]
    d_model = inputs.shape[1]

    small_parts = (
        norm_gain,
        ffn_gain,
        conv_inner,
        conv_inner_bias,
        mixer_gain,
        conv_state,
        conv_state_bias,
    )
    small = jnp.concatenate([a.reshape(-1) for a in small_parts] + [state_in.reshape(-1)])
    n_small = small.shape[0] - state_in.size
    both = join_tensor(small.reshape(1, -1), part)
    state_rows = both[:, n_small:].reshape(rows, state_cols)
    small_cols = -(-n_parts * n_small // rows)
    small_block = jnp.pad(
        both[:, :n_small].reshape(-1), (0, rows * small_cols - n_parts * n_small)
    ).reshape(rows, small_cols)
    step_cols = -(-(n_heads + small_cols) // 128) * 128
    step_block = jnp.pad(
        jnp.concatenate([step_in, small_block], 1),
        ((0, 0), (0, step_cols - n_heads - small_cols)),
    )
    front = jnp.concatenate(
        [
            mix_in[..., :head_dim].reshape(rows, inner),
            mix_in[..., head_dim:].reshape(rows, inner),
            attn_in.reshape(rows, qkv_cols),
            state_rows,
            step_block,
        ],
        1,
    )
    back = jnp.concatenate(
        [
            mixer_out.reshape(inner, rows).T,
            attn_out.reshape(attn_cols, rows).T,
            ffn_in.reshape(rows, 2 * hid),
            ffn_down.T,
        ],
        1,
    )
    x_at, qkv_at = inner, 2 * inner
    bc_at = qkv_at + qkv_cols
    step_at = bc_at + state_cols
    front_full = gather_rows(front, factors, coords)
    front_full, back = lax.optimization_barrier((front_full, back))
    back_full = gather_rows(back, factors, coords)
    mixout_t = back_full[:, :inner]
    attnout_t = back_full[:, inner : inner + attn_cols]
    ffin_full = back_full[:, inner + attn_cols : inner + attn_cols + 2 * hid]
    down_t = back_full[:, inner + attn_cols + 2 * hid :]

    smalls = front_full.reshape(n_dp, rows, -1)[
        :, :, step_at + n_heads : step_at + n_heads + small_cols
    ]
    smalls = smalls.reshape(n_dp, -1)[:, : n_parts * n_small].reshape(n_dp * n_parts, n_small)
    smalls = smalls.astype(F32)
    pieces = []
    at = 0
    for item in small_parts:
        piece = smalls[:, at : at + item.size].reshape((-1,) + item.shape)
        at += item.size
        if item.ndim == 2:
            piece = piece.transpose(1, 0, 2).reshape(item.shape[0], -1)
        else:
            piece = piece.reshape(-1)
        pieces.append(piece)
    gain_first, gain_second, conv_full, conv_bias_full, gain_mix_full, conv_bc, conv_bc_bias = pieces

    def local_cols(array, axis_dim):
        return lax.dynamic_slice_in_dim(array, part * inner, inner, axis_dim)

    def widen(local, axis_dim):
        full_shape = list(local.shape)
        full_shape[axis_dim] = inner * n_parts
        return lax.dynamic_update_slice_in_dim(
            jnp.zeros(full_shape, F32), local, part * inner, axis_dim
        )

    conv_local = local_cols(conv_full, 1)
    conv_bias_local = local_cols(conv_bias_full, 0)
    gain_mixer = local_cols(gain_mix_full, 0)

    cot_full = join_tensor(cotangent, part)
    inputs_f = inputs.astype(F32)
    inv_first = lax.rsqrt(jnp.mean(inputs_f * inputs_f, -1, keepdims=True) + EPS)
    unit_first = inputs_f * inv_first
    normed = join_tensor((unit_first * gain_first[None, :]).astype(BF16), part)

    row_index = jnp.arange(n_rows, dtype=jnp.int32)
    places = place * n_rows + row_index - segments
    half_dim = ADIM // 2
    freqs = ROPE_BASE ** (-2.0 * jnp.arange(half_dim, dtype=F32) / ADIM)
    angles = places.astype(F32)[:, None] * freqs[None, :]
    cosine, sine = jnp.cos(angles), jnp.sin(angles)
    n_taps = conv_inner.shape[0]
    same_doc = [(places >= n_taps - 1 - k).astype(F32) for k in range(n_taps - 1)]

    proj = dot(normed, front_full, ((1,), (0,)))

    def mixer(*values):
        return mamba_core(*values, segments, same_doc)

    mamba_value, mamba_pull = jax.vjp(
        mixer,
        proj[:, :inner],
        proj[:, x_at:qkv_at],
        proj[:, step_at : step_at + n_heads],
        proj[:, bc_at:step_at],
        conv_local,
        conv_bias_local,
        conv_bc,
        conv_bc_bias,
        decay_log,
        step_bias,
        skip_gain,
        gain_mixer,
    )
    mamba_low = mamba_value.astype(BF16)
    scaling = ADIM ** (-0.5)
    q_cols = QPK * ADIM
    q_part = proj[:, qkv_at : qkv_at + q_cols].reshape(n_rows, QPK, ADIM)
    k_part = proj[:, qkv_at + q_cols : qkv_at + q_cols + ADIM]
    queries = rotate(q_part, cosine, sine).astype(BF16)
    keys = rotate(k_part, cosine, sine).astype(BF16)
    vals = proj[:, qkv_at + q_cols + ADIM : bc_at].astype(BF16)
    blocks = query_blocks(segments)
    attended, norms = attend_forward(queries, keys, vals, blocks, scaling)
    attended_low = attended.reshape(n_rows, attn_cols).astype(BF16)
    mix_low = jnp.concatenate([mamba_low, attended_low], 1)
    out_t = back_full[:, : inner + attn_cols]
    mixed = split_tensor(dot(mix_low, out_t, ((1,), (1,))), part)
    middle = inputs_f + mixed
    inv_second = lax.rsqrt(jnp.mean(middle * middle, -1, keepdims=True) + EPS)
    unit_second = middle * inv_second
    hidden = join_tensor((unit_second * gain_second[None, :]).astype(BF16), part)
    gate_up = dot(hidden, ffin_full, ((1,), (0,)))
    gate = gate_up[:, :hid]
    upper = gate_up[:, hid:]
    sigma = jax.nn.sigmoid(gate)
    active = (gate * sigma * upper).astype(BF16)
    ffn_value = split_tensor(dot(active, down_t, ((1,), (1,))), part)
    output = (middle + ffn_value).astype(BF16)

    grad_down = dot(cot_full, active, ((0,), (0,)))
    grad_active = dot(cot_full, down_t, ((1,), (0,)))
    grad_gate = grad_active * upper * sigma * (1.0 + gate * (1.0 - sigma))
    grad_up = grad_active * gate * sigma
    grad_gu = jnp.concatenate([grad_gate.astype(BF16), grad_up.astype(BF16)], 1)
    grad_ffin = dot(hidden, grad_gu, ((0,), (0,)))
    ffn_sum = scatter_rows(
        jnp.concatenate([grad_ffin.astype(BF16), grad_down.astype(BF16)], 1), factors, coords
    ).astype(F32)
    grad_hidden = split_tensor(dot(grad_gu, ffin_full, ((1,), (1,))), part)
    grad_gain_second = jnp.sum(grad_hidden * unit_second, 0)
    grad_middle = cotangent.astype(F32) + norm_back(
        grad_hidden, unit_second, inv_second, gain_second
    )
    grad_mixed = join_tensor(grad_middle.astype(BF16), part)
    out_sum = scatter_rows(
        dot(grad_mixed, mix_low, ((0,), (0,))).astype(BF16), factors, coords
    ).astype(F32)
    grad_att = dot(grad_mixed, attnout_t, ((1,), (0,))).astype(BF16)
    grad_mamba = dot(grad_mixed, mixout_t, ((1,), (0,)))
    grad_q, grad_k, grad_v = attend_backward(
        queries, keys, vals, blocks, norms, grad_att.reshape(n_rows, QPK, ADIM), scaling
    )
    grad_q = rotate(grad_q, cosine, -sine).reshape(n_rows, q_cols)
    grad_k = rotate(grad_k, cosine, -sine)
    (
        grad_z,
        grad_x,
        grad_step,
        grad_bc,
        grad_conv,
        grad_conv_bias,
        grad_conv_bc,
        grad_conv_bc_bias,
        grad_decay,
        grad_step_bias,
        grad_skip,
        grad_gain_mix,
    ) = mamba_pull(grad_mamba)
    grad_proj = jnp.concatenate(
        [
            grad_z.astype(BF16),
            grad_x.astype(BF16),
            grad_q.astype(BF16),
            grad_k.astype(BF16),
            grad_v.astype(BF16),
            grad_bc.astype(BF16),
            grad_step.astype(BF16),
            jnp.zeros((n_rows, step_cols - n_heads), BF16),
        ],
        1,
    )
    front_sum = scatter_rows(
        dot(normed, grad_proj, ((0,), (0,))).astype(BF16), factors, coords
    ).astype(F32)
    grad_normed = split_tensor(dot(grad_proj, front_full, ((1,), (1,))), part)
    grad_gain_first = jnp.sum(grad_normed * unit_first, 0)
    inputs_grad = grad_middle + norm_back(grad_normed, unit_first, inv_first, gain_first)

    small_grads = (
        grad_gain_first,
        grad_gain_second,
        widen(grad_conv, 1),
        widen(grad_conv_bias, 0),
        widen(grad_gain_mix, 0),
        grad_conv_bc,
        grad_conv_bc_bias,
    )
    columns = []
    for item, grad in zip(small_parts, small_grads):
        if item.ndim == 2:
            piece = grad.reshape(item.shape[0], n_dp * n_parts, -1).transpose(1, 0, 2)
        else:
            piece = grad
        columns.append(piece.reshape(n_dp * n_parts, -1))
    piece_rows = jnp.concatenate(columns, 1).reshape(n_dp, n_parts * n_small)
    heads = jnp.concatenate([grad_decay, grad_step_bias, grad_skip])
    filled = n_parts * n_small + heads.shape[0]
    lines = -(-filled // 1024) * 8
    packed = jnp.concatenate(
        [
            piece_rows,
            jnp.broadcast_to(heads[None, :], (n_dp, heads.shape[0])),
            jnp.zeros((n_dp, lines * 128 - filled), F32),
        ],
        1,
    ).reshape(tuple(factors) + (lines, 128))
    for axis in range(len(factors)):
        packed = reduce_axis(packed, factors, axis, coords[axis])
    packed = packed.reshape(-1)
    pair = packed[: n_parts * n_small].reshape(n_parts, n_small)
    mine = lax.dynamic_index_in_dim(pair, part, 0, keepdims=False) + swap(
        lax.dynamic_index_in_dim(pair, 1 - part, 0, keepdims=False)
    )
    small_out = []
    at = 0
    for item in small_parts:
        small_out.append(mine[at : at + item.size].reshape(item.shape))
        at += item.size
    head_sums = packed[n_parts * n_small : filled].reshape(3, n_heads)

    state_sum = front_sum[:, bc_at:step_at]
    half = rows // n_parts
    state_grad = lax.dynamic_slice_in_dim(state_sum, part * half, half, 0) + swap(
        lax.dynamic_slice_in_dim(state_sum, (1 - part) * half, half, 0)
    )
    mix_grad = jnp.concatenate(
        [
            front_sum[:, :inner].reshape(rows, n_heads, head_dim),
            front_sum[:, x_at:qkv_at].reshape(rows, n_heads, head_dim),
        ],
        -1,
    )
    return (
        output,
        inputs_grad,
        small_out[0],
        mix_grad,
        front_sum[:, step_at : step_at + n_heads],
        state_grad,
        small_out[2],
        small_out[3],
        small_out[5],
        small_out[6],
        head_sums[0],
        head_sums[1],
        head_sums[2],
        small_out[4],
        front_sum[:, qkv_at:bc_at].reshape(attn_in.shape),
        out_sum[:, :inner].T.reshape(mixer_out.shape),
        out_sum[:, inner:].T.reshape(attn_out.shape),
        small_out[1],
        ffn_sum[:, : 2 * hid].reshape(ffn_in.shape),
        ffn_sum[:, 2 * hid :].T,
    )


def solution(mesh):
    return jax.shard_map(
        per_device,
        mesh=mesh,
        in_specs=(
            P(("dp", "tensor"), None),
            P("dp"),
            P(("dp", "tensor"), None),
            P(("dp", "tensor")),
            P("dp", "tensor", None),
            P("dp", "tensor"),
            P(("dp", "tensor"), None),
            P(None, ("dp", "tensor")),
            P(("dp", "tensor")),
            P(None, ("dp", "tensor")),
            P(("dp", "tensor")),
            P("tensor"),
            P("tensor"),
            P("tensor"),
            P(("dp", "tensor")),
            P("dp", "tensor", None),
            P("tensor", None, "dp"),
            P("tensor", None, "dp"),
            P(("dp", "tensor")),
            P("dp", None, "tensor"),
            P("tensor", "dp"),
        ),
        out_specs=(
            P(("dp", "tensor"), None),
            P(("dp", "tensor"), None),
            P(("dp", "tensor")),
            P("dp", "tensor", None),
            P("dp", "tensor"),
            P(("dp", "tensor"), None),
            P(None, ("dp", "tensor")),
            P(("dp", "tensor")),
            P(None, ("dp", "tensor")),
            P(("dp", "tensor")),
            P("tensor"),
            P("tensor"),
            P("tensor"),
            P(("dp", "tensor")),
            P("dp", "tensor", None),
            P("tensor", None, "dp"),
            P("tensor", None, "dp"),
            P(("dp", "tensor")),
            P("dp", None, "tensor"),
            P("tensor", "dp"),
        ),
        check_vma=False,
    )
```

time: 1980 us -> 833 us (0.42)
  waiting for transfers between devices: 1120 us -> 177 us
  blocking collectives: 365 us -> 0 us
  starting transfers between devices: 2.27 us -> 184 us
  matrix products: 232 us -> 158 us
  other arithmetic: 113 us -> 153 us
    reduce_scatter x9 -> x0, waiting for transfers between devices: 716 us -> none  [the longest x1 177 us: per_device(): lax.psum_scatter(grad_ffin, 'dp', scatter_dimension=0, tiled=True)]
    all_gather x6 -> x0, blocking collectives: 240 us -> none  [the longest x1 42.8 us: per_device(): lax.all_gather(state_in, ('dp', 'tensor'), axis=0, tiled=True)]
    unnamed x25 -> x0, waiting for transfers between devices: 233 us -> none
    ppermute x0 -> x99, starting transfers between devices: none -> 184 us  [the longest x21 101 us: reduce_axis(): lax.ppermute(send_up, 'dp', pairs_of(factors, axis, lambda c: c < step, l...]
    ppermute x0 -> x99, waiting for transfers between devices: none -> 177 us  [the longest x8 67.3 us: gather_axis(): lax.ppermute(block, 'dp', pairs_of(factors, axis, lambda c: True, lambda...]
    all_gather x8 -> x0, waiting for transfers between devices: 166 us -> none  [the longest x1 75.8 us: per_device(): lax.all_gather(ffn_in, 'dp', axis=0, tiled=True)]
    unnamed x2 -> x0, blocking collectives: 83.3 us -> none
    dot_general x49 -> x39, matrix products: 230 us -> 158 us  [the longest x13 73.9 us: dot(): return lax.dot_general(a, b, (dims, ((), ())), preferred_element_type=F32)]
  transfers between devices with their start and end apart: 21 -> 99, of which waited for: 16 -> 38; matrix products, arithmetic and copies ran while one was open for 10% -> 45% of each run, Pallas kernels for 0% -> 0%
where the time goes in v1:
time: 833 us; the launch traced here: 821 us
  starting transfers between devices  184 us (22%)
  waiting for transfers between devices  177 us (21%)
  matrix products  158 us (19%)
  other arithmetic  153 us (18%)
  local copies, waits for them, and re-layouts  144 us (17%)
    ppermute x21, starting transfers between devices, reduce_axis(): lax.ppermute(send_up, 'dp', pairs_of(factors, axis, lambda c: c < step, l...  101 us
    dot_general x13, matrix products, dot(): return lax.dot_general(a, b, (dims, ((), ())), preferred_element_type=F32)  73.9 us
    ppermute x8, waiting for transfers between devices, gather_axis(): lax.ppermute(block, 'dp', pairs_of(factors, axis, lambda c: True, lambda...  67.3 us
    ppermute x14, waiting for transfers between devices, reduce_axis(): lax.ppermute(pick(1 - coord), 'dp', pairs_of(factors, axis, lambda c: Tru...  44.5 us
    unnamed x422, local copies, waits for them, and re-layouts  36.1 us
    dot_general x3, matrix products, ssd_scan(): y_inner = jnp.einsum('chts,chsp->chtp', weights_ts, x_step, precision=PREC)  32.9 us
    ppermute x12, waiting for transfers between devices, gather_axis(): lax.ppermute(downward, 'dp', pairs_of(factors, axis, lambda c: 1 <= c <=...  27.5 us
    ppermute x12, starting transfers between devices, gather_axis(): lax.ppermute(upward, 'dp', pairs_of(factors, axis, lambda c: step - 1 <=...  19.5 us
  transfers between devices with their start and end apart: 99, of which 38 were waited for; matrix products, arithmetic and copies ran while one was open for 45% of the time, Pallas kernels for 0%

profile of v1, /device:TPU:0, one launch (start us, length us, event | category | flops | bytes accessed | tf_op | source)
XLA Modules:
  0.0 821.0 jit_solution(4818522531974679617)
XLA Ops:
  14.9 4.5 collective-permute-start.9
  37.3 9.5 %collective-permute-done.5 = bf16[1,1,1,32,2304]{4,3,2,1,0:T(8,128)(2,1)S(1)} collective-permute-done((bf16[1,1,1,32,2304]{4,3,2,1,0:T(8,128)(2,1)S(1)}, bf16[1,1,1,32,2304]{4,3,2,1,0:T(8,128)(2,1)S(1)}, u32[]{:S(2)}, u32[]{:S(2)}) %collective-permute-start.5) | collective-permute-done | bytes 147488 | tf_op jit(solution)/shard_map/ppermute | solution.py:73
  50.6 4.1 collective-permute-done.6
  58.0 7.2 collective-permute-done.7
  67.3 5.4 collective-permute-done.15
  76.6 18.1 %collective-permute-done.8 = bf16[4,2,1,32,2304]{4,3,2,1,0:T(8,128)(2,1)S(1)} collective-permute-done((bf16[4,2,1,32,2304]{4,3,2,1,0:T(8,128)(2,1)S(1)}, bf16[4,2,1,32,2304]{4,3,2,1,0:T(8,128)(2,1)S(1)}, u32[]{:S(2)}, u32[]{:S(2)}) %collective-permute-start.8) | collective-permute-done | bytes 1179680 | tf_op jit(solution)/shard_map/ppermute | solution.py:60
  130.3 3.9 collective-permute-done.30
  152.2 6.7 fusion.280
  167.7 3.8 fusion.57
  175.0 5.1 reshape.719
  183.4 4.0 fusion.66
  191.0 8.5 %fusion.55 = f32[4,256,12,64]{1,3,2,0:T(8,128)S(1)} fusion(f32[4,12,64,256]{3,2,1,0:T(8,128)S(1)} %fusion.129, f32[4,12,256]{2,1,0:T(8,128)S(1)} %fusion.171, f32[4,256,256]{2,1,0:T(8,128)S(1)} %fusion.282, pred[4,256,256]{2,1,0:T(8,128)(4,1)S(1)} %copy-done.96, f32[4,256,12,64]{1,0,3,2:T(4,128)S(1)} %copy-done.11, f32[4,256,12]{1,2,0:T(8,128)S(1)} %bitcast.415, ...), kind=kOutput, calls=%fused_computation.119 | convolution fusion | flops 1219756032 | bytes 10895360 | tf_op jit(solution)/shard_map/jvp(chts,chsp->chtp)/dot_general | solution.py:216
  203.9 3.7 copy.361
  244.9 36.6 %collective-permute-done.25 = bf16[4,2,1,32,4096]{4,3,2,1,0:T(8,128)(2,1)S(1)} collective-permute-done((bf16[4,2,1,32,4096]{4,3,2,1,0:T(8,128)(2,1)S(1)}, bf16[4,2,1,32,4096]{4,3,2,1,0:T(8,128)(2,1)S(1)}, u32[]{:S(2)}, u32[]{:S(2)}) %collective-permute-start.25) | collective-permute-done | bytes 2097184 | tf_op jit(solution)/shard_map/ppermute | solution.py:60
  281.4 3.7 fusion.25
  285.1 3.6 fusion.23
  288.8 7.8 pad_maximum_fusion
  296.6 4.6 fusion.97
  313.4 4.9 fusion.86
  320.3 3.7 fusion.88
  324.0 6.9 fusion.36
  331.0 5.3 multiply_convert_fusion.1
  336.3 8.5 %convolution_convert_fusion.1 = bf16[1024,2048]{1,0:T(8,128)(2,1)} fusion(bf16[1024,1024]{1,0:T(8,128)(2,1)S(1)} %fusion.88, bf16[1024,1024]{1,0:T(8,128)(2,1)} %get-tuple-element.197, bf16[1024,1024]{1,0:T(8,128)(2,1)S(1)} %get-tuple-element.196), kind=kOutput, calls=%fused_computation.63 | convolution fusion | flops 4305453056 | bytes 10485760 | tf_op jit(solution)/shard_map/dot_general | solution.py:342
  344.9 6.3 fusion.34
  351.2 3.8 convolution_convert_fusion.2
  364.0 4.0 fusion.106
  373.2 4.3 fusion.261
  378.2 19.1 %collective-permute-done.83 = bf16[4,2,1,32,3072]{4,3,2,1,0:T(8,128)(2,1)} collective-permute-done((bf16[4,2,1,32,3072]{4,3,2,1,0:T(8,128)(2,1)}, bf16[4,2,1,32,3072]{4,3,2,1,0:T(8,128)(2,1)}, u32[]{:S(2)}, u32[]{:S(2)}) %collective-permute-start.83) | collective-permute-done | bytes 1572896 | tf_op jit(solution)/shard_map/ppermute | solution.py:111
  402.7 5.4 collective-permute-done.91
  417.1 3.9 convolution_convert_fusion.3
  421.0 4.3 multiply_reduce_fusion.2
  425.3 7.1 multiply_reduce_fusion.1
  432.4 3.7 copy.372
  436.0 5.2 reshape.727
  441.2 3.9 fusion.63
  447.3 13.9 %fusion.9 = (f32[4,12,256]{2,1,0:T(8,128)}, f32[4,12,256]{2,1,0:T(8,128)}, f32[4,256,256]{2,1,0:T(8,128)}) fusion(f32[4,12,256]{2,1,0:T(8,128)S(1)} %fusion.171, f32[4,256,256]{2,1,0:T(8,128)S(1)} %copy-done.80, pred[4,256,256]{2,1,0:T(8,128)(4,1)S(1)} %copy-done.97, f32[4,256,12,64]{1,0,3,2:T(4,128)S(1)} %copy-done.12, f32[4,12,256]{2,1,0:T(8,128)S(1)} %copy.359, ...), kind=kOutput, calls=%fused_computation.17 | convolution fusion | flops 1236770816 | bytes 8847360 | tf_op jit(solution)/shard_map/transpose(jvp(chts,chsp->chtp))/dot_general | solution.py:216
  481.9 10.5 %fusion.51 = (f32[4,256,12,64]{1,3,2,0:T(8,128)}, f32[4,12,256,64]{2,3,1,0:T(8,128)S(1)}) fusion(f32[4,12,64,256]{3,2,1,0:T(8,128)} %fusion.119, f32[4,256,12]{1,2,0:T(8,128)} %copy.375, f32[4,256,12]{1,2,0:T(8,128)} %bitcast.401, f32[4,256,12,64]{1,0,3,2:T(4,128)} %reshape.727, f32[4,12,256]{2,1,0:T(8,128)S(1)} %fusion.171, ...), kind=kOutput, calls=%fused_computation.112 | convolution fusion | flops 1219756032 | bytes 14041088 | tf_op jit(solution)/shard_map/transpose(jvp(chts,chsp->chtp))/dot_general | solution.py:216
  492.4 4.0 fusion.49
  512.0 5.4 fusion.5
  529.3 3.9 copy.376
  539.2 9.5 %multiply_reduce_fusion.6 = (f32[768]{0:T(1024)S(1)}, f32[768]{0:T(1024)S(1)}, f32[768]{0:T(1024)S(1)}, f32[768]{0:T(1024)}, f32[768]{0:T(1024)S(1)}, /*index=5*/f32[1024,768]{1,0:T(8,128)S(1)}) fusion(f32[1024,768]{1,0:T(8,128)} %copy-done.10, f32[1024]{0:T(1024)S(1)} %copy-done.105, f32[1024]{0:T(1024)S(1)} %copy-done.103, f32[1024]{0:T(1024)S(1)} %copy-done.101, ...), kind=kLoop, calls=%fused_computation.128 | loop fusion | flops 18084096 | bytes 18905088 | tf_op jit(solution)/shard_map/transpose(jvp())/reduce_sum | solution.py:189
  556.0 7.5 concatenate.162
  563.5 8.6 %convolution_convert_fusion = bf16[1024,2304]{1,0:T(8,128)(2,1)S(1)} fusion(bf16[1024,1024]{1,0:T(8,128)(2,1)} %copy-done.60, bf16[1024,2304]{1,0:T(8,128)(2,1)} %concatenate.162), kind=kOutput, calls=%fused_computation.37 | convolution fusion | flops 4834197504 | bytes 11534336 | tf_op jit(solution)/shard_map/dot_general | solution.py:342
  572.1 9.1 %fusion.283 = f32[1024,1024]{1,0:T(8,128)} fusion(bf16[1024,2304]{1,0:T(8,128)(2,1)S(1)} %copy-done.44, bf16[1024,2304]{1,0:T(8,128)(2,1)} %bitcast.384), kind=kOutput, calls=%fused_computation.609 | convolution fusion | flops 4831838208 | bytes 13631488 | tf_op jit(solution)/shard_map/dot_general | solution.py:342
  607.7 4.4 collective-permute-start.93
  617.3 4.4 collective-permute-start.86
  626.5 4.4 collective-permute-start.94
  642.0 4.4 collective-permute-start.69
  648.2 4.3 collective-permute-start.77
  656.5 9.7 %collective-permute-start.70 = (bf16[1,1,1,32,1024]{4,3,2,1,0:T(8,128)(2,1)S(1)}, bf16[1,1,1,32,1024]{4,3,2,1,0:T(8,128)(2,1)S(1)}, u32[]{:S(2)}, u32[]{:S(2)}) collective-permute-start(bf16[1,1,1,32,1024]{4,3,2,1,0:T(8,128)(2,1)S(1)} %add_convert_fusion.44), channel_id=1, source_target_pairs={{0,8},{2,10},{4,12},{6,14},{8,16},{10,18},{12,20},{14,22},{1,9},{3... | collective-permute-start | bytes 196616 | tf_op jit(solution)/shard_map/ppermute | solution.py:122
  668.1 4.3 collective-permute-start.78
  678.2 13.2 %collective-permute-start.71 = (bf16[1,1,1,32,1024]{4,3,2,1,0:T(8,128)(2,1)}, bf16[1,1,1,32,1024]{4,3,2,1,0:T(8,128)(2,1)}, u32[]{:S(2)}, u32[]{:S(2)}) collective-permute-start(bf16[1,1,1,32,1024]{4,3,2,1,0:T(8,128)(2,1)} %get-tuple-element.256), channel_id=1, source_target_pairs={{0,8},{2,10},{4,12},{6,14},{8,16},{10,18},{12,20},{14,22},{16,24},... | collective-permute-start | bytes 196616 | tf_op jit(solution)/shard_map/ppermute | solution.py:122
  697.3 4.5 fusion.80
  701.8 4.6 collective-permute-start.79
  708.6 4.6 collective-permute-start.95
  716.8 4.4 collective-permute-start.42
  727.6 5.4 collective-permute-done.90
  734.8 9.2 %collective-permute-start.43 = (f32[1,2,2,8,128]{4,3,2,1,0:T(8,128)S(1)}, f32[1,2,2,8,128]{4,3,2,1,0:T(8,128)S(1)}, u32[]{:S(2)}, u32[]{:S(2)}) collective-permute-start(f32[1,2,2,8,128]{4,3,2,1,0:T(8,128)S(1)} %get-tuple-element.266), channel_id=1, source_target_pairs={{0,8},{2,10},{4,12},{6,14},{8,16},{10,18},{12,20},{14,22},{16,24},... | collective-permute-start | bytes 49160 | tf_op jit(solution)/shard_map/ppermute | solution.py:122
  766.8 12.0 %collective-permute-done.51 = bf16[4,1,1,32,2304]{4,3,2,1,0:T(8,128)(2,1)S(1)} collective-permute-done((bf16[4,1,1,32,2304]{4,3,2,1,0:T(8,128)(2,1)S(1)}, bf16[4,1,1,32,2304]{4,3,2,1,0:T(8,128)(2,1)S(1)}, u32[]{:S(2)}, u32[]{:S(2)}) %collective-permute-start.51) | collective-permute-done | bytes 589856 | tf_op jit(solution)/shard_map/ppermute | solution.py:111
  779.0 3.8 collective-permute-start.52
  786.5 4.4 collective-permute-start.53
  795.7 5.0 collective-permute-start.54
  801.5 5.2 collective-permute-start.62
  809.4 5.0 collective-permute-done.57
  (897 shorter events, 386.2 us)
Async XLA Ops:
  14.9 11.3 %collective-permute-start.9 = (bf16[1,1,1,32,2304]{4,3,2,1,0:T(8,128)(2,1)S(1)}, bf16[1,1,1,32,2304]{4,3,2,1,0:T(8,128)(2,1)S(1)}, u32[]{:S(2)}, u32[]{:S(2)}) collective-permute-start(bf16[1,1,1,32,2304]{4,3,2,1,0:T(8,128)(2,1)S(1)} %get-tuple-element.251), channel_id=1, source_target_pairs={{0,8},{2,10},{4,12},{6,14},{8,16},{10,18},{12,20},{14,22},{16,24},... | collective-permute-start | bytes 442376 | tf_op jit(solution)/shard_map/ppermute | solution.py:68
  20.1 10.1 %collective-permute-start.1 = (bf16[1,1,1,32,2304]{4,3,2,1,0:T(8,128)(2,1)S(1)}, bf16[1,1,1,32,2304]{4,3,2,1,0:T(8,128)(2,1)S(1)}, u32[]{:S(2)}, u32[]{:S(2)}) collective-permute-start(bf16[1,1,1,32,2304]{4,3,2,1,0:T(8,128)(2,1)S(1)} %get-tuple-element.250), channel_id=1, source_target_pairs={{0,8},{2,10},{4,12},{6,14},{8,16},{10,18},{12,20},{14,22},{16,24},... | collective-permute-start | bytes 442376 | tf_op jit(solution)/shard_map/ppermute | solution.py:68
  23.6 8.6 %collective-permute-start.4 = (bf16[1,1,1,32,2304]{4,3,2,1,0:T(8,128)(2,1)S(1)}, bf16[1,1,1,32,2304]{4,3,2,1,0:T(8,128)(2,1)S(1)}, u32[]{:S(2)}, u32[]{:S(2)}) collective-permute-start(bf16[1,1,1,32,2304]{4,3,2,1,0:T(8,128)(2,1)S(1)} %get-tuple-element.250), channel_id=1, source_target_pairs={{8,0},{10,2},{12,4},{14,6},{16,8},{18,10},{20,12},{22,14},{24,16},... | collective-permute-start | bytes 442376 | tf_op jit(solution)/shard_map/ppermute | solution.py:73
  24.9 9.4 %collective-permute-start.12 = (bf16[1,1,1,32,2304]{4,3,2,1,0:T(8,128)(2,1)S(1)}, bf16[1,1,1,32,2304]{4,3,2,1,0:T(8,128)(2,1)S(1)}, u32[]{:S(2)}, u32[]{:S(2)}) collective-permute-start(bf16[1,1,1,32,2304]{4,3,2,1,0:T(8,128)(2,1)S(1)} %get-tuple-element.251), channel_id=1, source_target_pairs={{8,0},{10,2},{12,4},{14,6},{16,8},{18,10},{20,12},{22,14},{24,16},... | collective-permute-start | bytes 442376 | tf_op jit(solution)/shard_map/ppermute | solution.py:73
  26.2 9.4 %collective-permute-start.10 = (bf16[1,1,1,32,2304]{4,3,2,1,0:T(8,128)(2,1)S(1)}, bf16[1,1,1,32,2304]{4,3,2,1,0:T(8,128)(2,1)S(1)}, u32[]{:S(2)}, u32[]{:S(2)}) collective-permute-start(bf16[1,1,1,32,2304]{4,3,2,1,0:T(8,128)(2,1)S(1)} %collective-permute-done.9), channel_id=1, source_target_pairs={{8,16},{10,18},{12,20},{14,22},{16,24},{18,26},{20,28},{22,30},{9,... | collective-permute-start | bytes 442376 | tf_op jit(solution)/shard_map/ppermute | solution.py:68
  32.2 14.5 %collective-permute-start.5 = (bf16[1,1,1,32,2304]{4,3,2,1,0:T(8,128)(2,1)S(1)}, bf16[1,1,1,32,2304]{4,3,2,1,0:T(8,128)(2,1)S(1)}, u32[]{:S(2)}, u32[]{:S(2)}) collective-permute-start(bf16[1,1,1,32,2304]{4,3,2,1,0:T(8,128)(2,1)S(1)} %collective-permute-done.4), channel_id=1, source_target_pairs={{8,0},{10,2},{12,4},{14,6},{16,8},{18,10},{20,12},{22,14},{9,1},{1... | collective-permute-start | bytes 442376 | tf_op jit(solution)/shard_map/ppermute | solution.py:73
  34.3 14.7 %collective-permute-start.13 = (bf16[1,1,1,32,2304]{4,3,2,1,0:T(8,128)(2,1)S(1)}, bf16[1,1,1,32,2304]{4,3,2,1,0:T(8,128)(2,1)S(1)}, u32[]{:S(2)}, u32[]{:S(2)}) collective-permute-start(bf16[1,1,1,32,2304]{4,3,2,1,0:T(8,128)(2,1)S(1)} %collective-permute-done.12), channel_id=1, source_target_pairs={{8,0},{10,2},{12,4},{14,6},{16,8},{18,10},{20,12},{22,14},{9,1},{1... | collective-permute-start | bytes 442376 | tf_op jit(solution)/shard_map/ppermute | solution.py:73
  35.6 14.7 %collective-permute-start.11 = (bf16[1,1,1,32,2304]{4,3,2,1,0:T(8,128)(2,1)S(1)}, bf16[1,1,1,32,2304]{4,3,2,1,0:T(8,128)(2,1)S(1)}, u32[]{:S(2)}, u32[]{:S(2)}) collective-permute-start(bf16[1,1,1,32,2304]{4,3,2,1,0:T(8,128)(2,1)S(1)} %collective-permute-done.10), channel_id=1, source_target_pairs={{16,24},{18,26},{20,28},{22,30},{17,25},{19,27},{21,29},{23,31}} | collective-permute-start | bytes 442376 | tf_op jit(solution)/shard_map/ppermute | solution.py:68
  36.6 13.8 %collective-permute-start.3 = (bf16[1,1,1,32,2304]{4,3,2,1,0:T(8,128)(2,1)S(1)}, bf16[1,1,1,32,2304]{4,3,2,1,0:T(8,128)(2,1)S(1)}, u32[]{:S(2)}, u32[]{:S(2)}) collective-permute-start(bf16[1,1,1,32,2304]{4,3,2,1,0:T(8,128)(2,1)S(1)} %collective-permute-done.2), channel_id=1, source_target_pairs={{16,24},{18,26},{20,28},{22,30},{17,25},{19,27},{21,29},{23,31}} | collective-permute-start | bytes 442376 | tf_op jit(solution)/shard_map/ppermute | solution.py:68
  54.7 10.5 %collective-permute-start.7 = (bf16[4,1,1,32,2304]{4,3,2,1,0:T(8,128)(2,1)S(1)}, bf16[4,1,1,32,2304]{4,3,2,1,0:T(8,128)(2,1)S(1)}, u32[]{:S(2)}, u32[]{:S(2)}) collective-permute-start(bf16[4,1,1,32,2304]{4,3,2,1,0:T(8,128)(2,1)S(1)} %constant_dynamic-slice_fusion.43), channel_id=1, source_target_pairs={{0,4},{2,6},{4,0},{6,2},{8,12},{10,14},{12,8},{14,10},{16,20},{18,... | collective-permute-start | bytes 1769480 | tf_op jit(solution)/shard_map/ppermute | solution.py:60
  56.4 16.3 %collective-permute-start.15 = (bf16[4,1,1,32,2304]{4,3,2,1,0:T(8,128)(2,1)S(1)}, bf16[4,1,1,32,2304]{4,3,2,1,0:T(8,128)(2,1)S(1)}, u32[]{:S(2)}, u32[]{:S(2)}) collective-permute-start(bf16[4,1,1,32,2304]{4,3,2,1,0:T(8,128)(2,1)S(1)} %constant_dynamic-slice_fusion.42), channel_id=1, source_target_pairs={{0,2},{2,0},{4,6},{6,4},{8,10},{10,8},{12,14},{14,12},{16,18},{18,... | collective-permute-start | bytes 1769480 | tf_op jit(solution)/shard_map/ppermute | solution.py:60
  65.8 28.9 %collective-permute-start.8 = (bf16[4,2,1,32,2304]{4,3,2,1,0:T(8,128)(2,1)S(1)}, bf16[4,2,1,32,2304]{4,3,2,1,0:T(8,128)(2,1)S(1)}, u32[]{:S(2)}, u32[]{:S(2)}) collective-permute-start(bf16[4,2,1,32,2304]{4,3,2,1,0:T(8,128)(2,1)S(1)} %fusion.142), channel_id=1, source_target_pairs={{0,2},{2,0},{4,6},{6,4},{8,10},{10,8},{12,14},{14,12},{16,18},{18,... | collective-permute-start | bytes 3538952 | tf_op jit(solution)/shard_map/ppermute | solution.py:60
  73.4 22.5 %collective-permute-start.16 = (bf16[4,1,2,32,2304]{4,3,2,1,0:T(8,128)(2,1)S(1)}, bf16[4,1,2,32,2304]{4,3,2,1,0:T(8,128)(2,1)S(1)}, u32[]{:S(2)}, u32[]{:S(2)}) collective-permute-start(bf16[4,1,2,32,2304]{4,3,2,1,0:T(8,128)(2,1)S(1)} %fusion.140), channel_id=1, source_target_pairs={{0,4},{2,6},{4,0},{6,2},{8,12},{10,14},{12,8},{14,10},{16,20},{18,... | collective-permute-start | bytes 3538952 | tf_op jit(solution)/shard_map/ppermute | solution.py:60
  101.0 8.2 collective-permute-start.26
  105.8 9.6 %collective-permute-start.21 = (bf16[1,1,1,32,4096]{4,3,2,1,0:T(8,128)(2,1)}, bf16[1,1,1,32,4096]{4,3,2,1,0:T(8,128)(2,1)S(1)}, u32[]{:S(2)}, u32[]{:S(2)}) collective-permute-start(bf16[1,1,1,32,4096]{4,3,2,1,0:T(8,128)(2,1)} %get-tuple-element.246), channel_id=1, source_target_pairs={{8,0},{10,2},{12,4},{14,6},{16,8},{18,10},{20,12},{22,14},{24,16},... | collective-permute-start | bytes 786440 | tf_op jit(solution)/shard_map/ppermute | solution.py:73
  107.1 11.1 %collective-permute-start.29 = (bf16[1,1,1,32,4096]{4,3,2,1,0:T(8,128)(2,1)}, bf16[1,1,1,32,4096]{4,3,2,1,0:T(8,128)(2,1)S(1)}, u32[]{:S(2)}, u32[]{:S(2)}) collective-permute-start(bf16[1,1,1,32,4096]{4,3,2,1,0:T(8,128)(2,1)} %get-tuple-element.247), channel_id=1, source_target_pairs={{8,0},{10,2},{12,4},{14,6},{16,8},{18,10},{20,12},{22,14},{24,16},... | collective-permute-start | bytes 786440 | tf_op jit(solution)/shard_map/ppermute | solution.py:73
  109.1 10.4 %collective-permute-start.27 = (bf16[1,1,1,32,4096]{4,3,2,1,0:T(8,128)(2,1)S(1)}, bf16[1,1,1,32,4096]{4,3,2,1,0:T(8,128)(2,1)}, u32[]{:S(2)}, u32[]{:S(2)}) collective-permute-start(bf16[1,1,1,32,4096]{4,3,2,1,0:T(8,128)(2,1)S(1)} %collective-permute-done.26), channel_id=1, source_target_pairs={{8,16},{10,18},{12,20},{14,22},{16,24},{18,26},{20,28},{22,30},{9,... | collective-permute-start | bytes 786440 | tf_op jit(solution)/shard_map/ppermute | solution.py:68
  110.8 38.0 %collective-permute-start.17 = (bf16[512,1024]{1,0:T(8,128)(2,1)S(1)}, bf16[512,1024]{1,0:T(8,128)(2,1)S(1)}, u32[]{:S(2)}, u32[]{:S(2)}) collective-permute-start(bf16[512,1024]{1,0:T(8,128)(2,1)S(1)} %fusion.76), channel_id=1, source_target_pairs={{0,1},{1,0},{2,3},{3,2},{4,5},{5,4},{6,7},{7,6},{8,9},{9,8},{10,11... | collective-permute-start | bytes 3145736 | tf_op jit(solution)/shard_map/ppermute | solution.py:149
  111.0 16.5 %collective-permute-start.19 = (bf16[1,1,1,32,4096]{4,3,2,1,0:T(8,128)(2,1)}, bf16[1,1,1,32,4096]{4,3,2,1,0:T(8,128)(2,1)}, u32[]{:S(2)}, u32[]{:S(2)}) collective-permute-start(bf16[1,1,1,32,4096]{4,3,2,1,0:T(8,128)(2,1)} %collective-permute-done.18), channel_id=1, source_target_pairs={{8,16},{10,18},{12,20},{14,22},{16,24},{18,26},{20,28},{22,30},{9,... | collective-permute-start | bytes 786440 | tf_op jit(solution)/shard_map/ppermute | solution.py:68
  115.4 13.6 %collective-permute-start.22 = (bf16[1,1,1,32,4096]{4,3,2,1,0:T(8,128)(2,1)S(1)}, bf16[1,1,1,32,4096]{4,3,2,1,0:T(8,128)(2,1)}, u32[]{:S(2)}, u32[]{:S(2)}) collective-permute-start(bf16[1,1,1,32,4096]{4,3,2,1,0:T(8,128)(2,1)S(1)} %collective-permute-done.21), channel_id=1, source_target_pairs={{8,0},{10,2},{12,4},{14,6},{16,8},{18,10},{20,12},{22,14},{9,1},{1... | collective-permute-start | bytes 786440 | tf_op jit(solution)/shard_map/ppermute | solution.py:73
  118.2 16.0 %collective-permute-start.30 = (bf16[1,1,1,32,4096]{4,3,2,1,0:T(8,128)(2,1)S(1)}, bf16[1,1,1,32,4096]{4,3,2,1,0:T(8,128)(2,1)}, u32[]{:S(2)}, u32[]{:S(2)}) collective-permute-start(bf16[1,1,1,32,4096]{4,3,2,1,0:T(8,128)(2,1)S(1)} %collective-permute-done.29), channel_id=1, source_target_pairs={{8,0},{10,2},{12,4},{14,6},{16,8},{18,10},{20,12},{22,14},{9,1},{1... | collective-permute-start | bytes 786440 | tf_op jit(solution)/shard_map/ppermute | solution.py:73
  119.5 16.5 %collective-permute-start.28 = (bf16[1,1,1,32,4096]{4,3,2,1,0:T(8,128)(2,1)}, bf16[1,1,1,32,4096]{4,3,2,1,0:T(8,128)(2,1)}, u32[]{:S(2)}, u32[]{:S(2)}) collective-permute-start(bf16[1,1,1,32,4096]{4,3,2,1,0:T(8,128)(2,1)} %collective-permute-done.27), channel_id=1, source_target_pairs={{16,24},{18,26},{20,28},{22,30},{17,25},{19,27},{21,29},{23,31}} | collective-permute-start | bytes 786440 | tf_op jit(solution)/shard_map/ppermute | solution.py:68
  127.5 10.5 %collective-permute-start.20 = (bf16[1,1,1,32,4096]{4,3,2,1,0:T(8,128)(2,1)}, bf16[1,1,1,32,4096]{4,3,2,1,0:T(8,128)(2,1)S(1)}, u32[]{:S(2)}, u32[]{:S(2)}) collective-permute-start(bf16[1,1,1,32,4096]{4,3,2,1,0:T(8,128)(2,1)} %collective-permute-done.19), channel_id=1, source_target_pairs={{16,24},{18,26},{20,28},{22,30},{17,25},{19,27},{21,29},{23,31}} | collective-permute-start | bytes 786440 | tf_op jit(solution)/shard_map/ppermute | solution.py:68
  129.0 12.3 %collective-permute-start.23 = (bf16[1,1,1,32,4096]{4,3,2,1,0:T(8,128)(2,1)}, bf16[1,1,1,32,4096]{4,3,2,1,0:T(8,128)(2,1)S(1)}, u32[]{:S(2)}, u32[]{:S(2)}) collective-permute-start(bf16[1,1,1,32,4096]{4,3,2,1,0:T(8,128)(2,1)} %collective-permute-done.22), channel_id=1, source_target_pairs={{8,0},{10,2},{12,4},{14,6},{9,1},{11,3},{13,5},{15,7}} | collective-permute-start | bytes 786440 | tf_op jit(solution)/shard_map/ppermute | solution.py:73
  134.2 12.0 %collective-permute-start.31 = (bf16[1,1,1,32,4096]{4,3,2,1,0:T(8,128)(2,1)}, bf16[1,1,1,32,4096]{4,3,2,1,0:T(8,128)(2,1)S(1)}, u32[]{:S(2)}, u32[]{:S(2)}) collective-permute-start(bf16[1,1,1,32,4096]{4,3,2,1,0:T(8,128)(2,1)} %collective-permute-done.30), channel_id=1, source_target_pairs={{8,0},{10,2},{12,4},{14,6},{9,1},{11,3},{13,5},{15,7}} | collective-permute-start | bytes 786440 | tf_op jit(solution)/shard_map/ppermute | solution.py:73
  142.4 89.4 %collective-permute-start.24 = (bf16[4,1,1,32,4096]{4,3,2,1,0:T(8,128)(2,1)}, bf16[4,1,1,32,4096]{4,3,2,1,0:T(8,128)(2,1)}, u32[]{:S(2)}, u32[]{:S(2)}) collective-permute-start(bf16[4,1,1,32,4096]{4,3,2,1,0:T(8,128)(2,1)} %constant_dynamic-slice_fusion.41), channel_id=1, source_target_pairs={{0,4},{2,6},{4,0},{6,2},{8,12},{10,14},{12,8},{14,10},{16,20},{18,... | collective-permute-start | bytes 3145736 | tf_op jit(solution)/shard_map/ppermute | solution.py:60
  147.3 87.7 %collective-permute-start.32 = (bf16[4,1,1,32,4096]{4,3,2,1,0:T(8,128)(2,1)}, bf16[4,1,1,32,4096]{4,3,2,1,0:T(8,128)(2,1)}, u32[]{:S(2)}, u32[]{:S(2)}) collective-permute-start(bf16[4,1,1,32,4096]{4,3,2,1,0:T(8,128)(2,1)} %constant_dynamic-slice_fusion.40), channel_id=1, source_target_pairs={{0,2},{2,0},{4,6},{6,4},{8,10},{10,8},{12,14},{14,12},{16,18},{18,... | collective-permute-start | bytes 3145736 | tf_op jit(solution)/shard_map/ppermute | solution.py:60
  234.4 47.0 %collective-permute-start.25 = (bf16[4,2,1,32,4096]{4,3,2,1,0:T(8,128)(2,1)S(1)}, bf16[4,2,1,32,4096]{4,3,2,1,0:T(8,128)(2,1)S(1)}, u32[]{:S(2)}, u32[]{:S(2)}) collective-permute-start(bf16[4,2,1,32,4096]{4,3,2,1,0:T(8,128)(2,1)S(1)} %fusion.92), channel_id=1, source_target_pairs={{0,2},{2,0},{4,6},{6,4},{8,10},{10,8},{12,14},{14,12},{16,18},{18,... | collective-permute-start | bytes 6291464 | tf_op jit(solution)/shard_map/ppermute | solution.py:60
  237.9 47.2 %collective-permute-start.33 = (bf16[4,1,2,32,4096]{4,3,2,1,0:T(8,128)(2,1)S(1)}, bf16[4,1,2,32,4096]{4,3,2,1,0:T(8,128)(2,1)S(1)}, u32[]{:S(2)}, u32[]{:S(2)}) collective-permute-start(bf16[4,1,2,32,4096]{4,3,2,1,0:T(8,128)(2,1)S(1)} %fusion.90), channel_id=1, source_target_pairs={{0,4},{2,6},{4,0},{6,2},{8,12},{10,14},{12,8},{14,10},{16,20},{18,... | collective-permute-start | bytes 6291464 | tf_op jit(solution)/shard_map/ppermute | solution.py:60
  304.4 9.0 %collective-permute-start.37 = (bf16[512,1024]{1,0:T(8,128)(2,1)}, bf16[512,1024]{1,0:T(8,128)(2,1)}, u32[]{:S(2)}, u32[]{:S(2)}) collective-permute-start(bf16[512,1024]{1,0:T(8,128)(2,1)} %param.23), channel_id=1, source_target_pairs={{0,1},{1,0},{2,3},{3,2},{4,5},{5,4},{6,7},{7,6},{8,9},{9,8},{10,11... | collective-permute-start | bytes 3145736 | tf_op jit(solution)/shard_map/ppermute | solution.py:149
  360.3 37.0 %collective-permute-start.83 = (bf16[4,2,1,32,3072]{4,3,2,1,0:T(8,128)(2,1)}, bf16[4,2,1,32,3072]{4,3,2,1,0:T(8,128)(2,1)}, u32[]{:S(2)}, u32[]{:S(2)}) collective-permute-start(bf16[4,2,1,32,3072]{4,3,2,1,0:T(8,128)(2,1)} %constant_dynamic-slice_fusion.7), channel_id=1, source_target_pairs={{0,2},{2,0},{4,6},{6,4},{8,10},{10,8},{12,14},{14,12},{16,18},{18,... | collective-permute-start | bytes 4718600 | tf_op jit(solution)/shard_map/ppermute | solution.py:111
  362.4 10.0 %collective-permute-start.38 = (bf16[512,1024]{1,0:T(8,128)(2,1)S(1)}, bf16[512,1024]{1,0:T(8,128)(2,1)S(1)}, u32[]{:S(2)}, u32[]{:S(2)}) collective-permute-start(bf16[512,1024]{1,0:T(8,128)(2,1)S(1)} %dynamic-slice_convert_fusion.1), channel_id=1, source_target_pairs={{0,1},{1,0},{2,3},{3,2},{4,5},{5,4},{6,7},{7,6},{8,9},{9,8},{10,11... | collective-permute-start | bytes 3145736 | tf_op jit(solution)/shard_map/ppermute | solution.py:149
  370.5 37.5 %collective-permute-start.91 = (bf16[4,1,2,32,3072]{4,3,2,1,0:T(8,128)(2,1)}, bf16[4,1,2,32,3072]{4,3,2,1,0:T(8,128)(2,1)}, u32[]{:S(2)}, u32[]{:S(2)}) collective-permute-start(bf16[4,1,2,32,3072]{4,3,2,1,0:T(8,128)(2,1)} %constant_dynamic-slice_fusion.3), channel_id=1, source_target_pairs={{0,4},{2,6},{4,0},{6,2},{8,12},{10,14},{12,8},{14,10},{16,20},{18,... | collective-permute-start | bytes 4718600 | tf_op jit(solution)/shard_map/ppermute | solution.py:111
  377.5 36.0 %collective-permute-start.39 = (bf16[512,1024]{1,0:T(8,128)(2,1)}, bf16[512,1024]{1,0:T(8,128)(2,1)}, u32[]{:S(2)}, u32[]{:S(2)}) collective-permute-start(bf16[512,1024]{1,0:T(8,128)(2,1)} %get-tuple-element.180), channel_id=1, source_target_pairs={{0,1},{1,0},{2,3},{3,2},{4,5},{5,4},{6,7},{7,6},{8,9},{9,8},{10,11... | collective-permute-start | bytes 3145736 | tf_op jit(solution)/shard_map/ppermute | solution.py:149
  400.8 199.3 %collective-permute-start.84 = (bf16[4,1,1,32,3072]{4,3,2,1,0:T(8,128)(2,1)}, bf16[4,1,1,32,3072]{4,3,2,1,0:T(8,128)(2,1)}, u32[]{:S(2)}, u32[]{:S(2)}) collective-permute-start(bf16[4,1,1,32,3072]{4,3,2,1,0:T(8,128)(2,1)} %constant_dynamic-slice_fusion.6), channel_id=1, source_target_pairs={{0,4},{2,6},{4,0},{6,2},{8,12},{10,14},{12,8},{14,10},{16,20},{18,... | collective-permute-start | bytes 2359304 | tf_op jit(solution)/shard_map/ppermute | solution.py:111
  412.2 189.6 %collective-permute-start.92 = (bf16[4,1,1,32,3072]{4,3,2,1,0:T(8,128)(2,1)}, bf16[4,1,1,32,3072]{4,3,2,1,0:T(8,128)(2,1)}, u32[]{:S(2)}, u32[]{:S(2)}) collective-permute-start(bf16[4,1,1,32,3072]{4,3,2,1,0:T(8,128)(2,1)} %constant_dynamic-slice_fusion.2), channel_id=1, source_target_pairs={{0,2},{2,0},{4,6},{6,4},{8,10},{10,8},{12,14},{14,12},{16,18},{18,... | collective-permute-start | bytes 2359304 | tf_op jit(solution)/shard_map/ppermute | solution.py:111
  582.3 33.0 %collective-permute-start.67 = (bf16[4,2,1,32,1024]{4,3,2,1,0:T(8,128)(2,1)}, bf16[4,2,1,32,1024]{4,3,2,1,0:T(8,128)(2,1)}, u32[]{:S(2)}, u32[]{:S(2)}) collective-permute-start(bf16[4,2,1,32,1024]{4,3,2,1,0:T(8,128)(2,1)} %constant_dynamic-slice_fusion.15), channel_id=1, source_target_pairs={{0,2},{2,0},{4,6},{6,4},{8,10},{10,8},{12,14},{14,12},{16,18},{18,... | collective-permute-start | bytes 1572872 | tf_op jit(solution)/shard_map/ppermute | solution.py:111
  584.0 33.3 %collective-permute-start.75 = (bf16[4,1,2,32,1024]{4,3,2,1,0:T(8,128)(2,1)}, bf16[4,1,2,32,1024]{4,3,2,1,0:T(8,128)(2,1)}, u32[]{:S(2)}, u32[]{:S(2)}) collective-permute-start(bf16[4,1,2,32,1024]{4,3,2,1,0:T(8,128)(2,1)} %constant_dynamic-slice_fusion.11), channel_id=1, source_target_pairs={{0,4},{2,6},{4,0},{6,2},{8,12},{10,14},{12,8},{14,10},{16,20},{18,... | collective-permute-start | bytes 1572872 | tf_op jit(solution)/shard_map/ppermute | solution.py:111
  588.9 172.5 %collective-permute-start.50 = (bf16[4,2,1,32,2304]{4,3,2,1,0:T(8,128)(2,1)}, bf16[4,2,1,32,2304]{4,3,2,1,0:T(8,128)(2,1)}, u32[]{:S(2)}, u32[]{:S(2)}) collective-permute-start(bf16[4,2,1,32,2304]{4,3,2,1,0:T(8,128)(2,1)} %constant_dynamic-slice_fusion.25), channel_id=1, source_target_pairs={{0,2},{2,0},{4,6},{6,4},{8,10},{10,8},{12,14},{14,12},{16,18},{18,... | collective-permute-start | bytes 3538952 | tf_op jit(solution)/shard_map/ppermute | solution.py:111
  600.1 164.0 %collective-permute-start.58 = (bf16[4,1,2,32,2304]{4,3,2,1,0:T(8,128)(2,1)}, bf16[4,1,2,32,2304]{4,3,2,1,0:T(8,128)(2,1)}, u32[]{:S(2)}, u32[]{:S(2)}) collective-permute-start(bf16[4,1,2,32,2304]{4,3,2,1,0:T(8,128)(2,1)} %constant_dynamic-slice_fusion.21), channel_id=1, source_target_pairs={{0,4},{2,6},{4,0},{6,2},{8,12},{10,14},{12,8},{14,10},{16,20},{18,... | collective-permute-start | bytes 3538952 | tf_op jit(solution)/shard_map/ppermute | solution.py:111
  615.3 76.8 %collective-permute-start.40 = (bf16[512,1024]{1,0:T(8,128)(2,1)S(1)}, bf16[512,1024]{1,0:T(8,128)(2,1)S(1)}, u32[]{:S(2)}, u32[]{:S(2)}) collective-permute-start(bf16[512,1024]{1,0:T(8,128)(2,1)S(1)} %dynamic-slice_convert_fusion), channel_id=1, source_target_pairs={{0,1},{1,0},{2,3},{3,2},{4,5},{5,4},{6,7},{7,6},{8,9},{9,8},{10,11... | collective-permute-start | bytes 3145736 | tf_op jit(solution)/shard_map/ppermute | solution.py:149
  617.3 9.2 %collective-permute-start.86 = (bf16[1,1,1,32,3072]{4,3,2,1,0:T(8,128)(2,1)S(1)}, bf16[1,1,1,32,3072]{4,3,2,1,0:T(8,128)(2,1)S(1)}, u32[]{:S(2)}, u32[]{:S(2)}) collective-permute-start(bf16[1,1,1,32,3072]{4,3,2,1,0:T(8,128)(2,1)S(1)} %add_convert_fusion.24), channel_id=1, source_target_pairs={{0,8},{2,10},{4,12},{6,14},{8,16},{10,18},{12,20},{14,22},{1,9},{3... | collective-permute-start | bytes 589832 | tf_op jit(solution)/shard_map/ppermute | solution.py:122
  623.0 8.7 %collective-permute-start.96 = (bf16[1,1,1,32,3072]{4,3,2,1,0:T(8,128)(2,1)S(1)}, bf16[1,1,1,32,3072]{4,3,2,1,0:T(8,128)(2,1)S(1)}, u32[]{:S(2)}, u32[]{:S(2)}) collective-permute-start(bf16[1,1,1,32,3072]{4,3,2,1,0:T(8,128)(2,1)S(1)} %get-tuple-element.231), channel_id=1, source_target_pairs={{24,16},{26,18},{28,20},{30,22},{25,17},{27,19},{29,21},{31,23}} | collective-permute-start | bytes 589832 | tf_op jit(solution)/shard_map/ppermute | solution.py:125
  626.5 8.4 %collective-permute-start.94 = (bf16[1,1,1,32,3072]{4,3,2,1,0:T(8,128)(2,1)S(1)}, bf16[1,1,1,32,3072]{4,3,2,1,0:T(8,128)(2,1)S(1)}, u32[]{:S(2)}, u32[]{:S(2)}) collective-permute-start(bf16[1,1,1,32,3072]{4,3,2,1,0:T(8,128)(2,1)S(1)} %add_convert_fusion.19), channel_id=1, source_target_pairs={{0,8},{2,10},{4,12},{6,14},{8,16},{10,18},{12,20},{14,22},{1,9},{3... | collective-permute-start | bytes 589832 | tf_op jit(solution)/shard_map/ppermute | solution.py:122
  639.4 15.7 %collective-permute-start.89 = (bf16[1,1,1,32,3072]{4,3,2,1,0:T(8,128)(2,1)S(1)}, bf16[1,1,1,32,3072]{4,3,2,1,0:T(8,128)(2,1)S(1)}, u32[]{:S(2)}, u32[]{:S(2)}) collective-permute-start(bf16[1,1,1,32,3072]{4,3,2,1,0:T(8,128)(2,1)S(1)} %get-tuple-element.225), channel_id=1, source_target_pairs={{16,8},{18,10},{20,12},{22,14},{24,16},{26,18},{28,20},{30,22},{17... | collective-permute-start | bytes 589832 | tf_op jit(solution)/shard_map/ppermute | solution.py:125
  655.1 11.8 %collective-permute-start.72 = (bf16[1,1,1,32,1024]{4,3,2,1,0:T(8,128)(2,1)S(1)}, bf16[1,1,1,32,1024]{4,3,2,1,0:T(8,128)(2,1)S(1)}, u32[]{:S(2)}, u32[]{:S(2)}) collective-permute-start(bf16[1,1,1,32,1024]{4,3,2,1,0:T(8,128)(2,1)S(1)} %get-tuple-element.259), channel_id=1, source_target_pairs={{24,16},{26,18},{28,20},{30,22},{25,17},{27,19},{29,21},{31,23}} | collective-permute-start | bytes 196616 | tf_op jit(solution)/shard_map/ppermute | solution.py:125
  656.5 11.6 %collective-permute-start.70 = (bf16[1,1,1,32,1024]{4,3,2,1,0:T(8,128)(2,1)S(1)}, bf16[1,1,1,32,1024]{4,3,2,1,0:T(8,128)(2,1)S(1)}, u32[]{:S(2)}, u32[]{:S(2)}) collective-permute-start(bf16[1,1,1,32,1024]{4,3,2,1,0:T(8,128)(2,1)S(1)} %add_convert_fusion.44), channel_id=1, source_target_pairs={{0,8},{2,10},{4,12},{6,14},{8,16},{10,18},{12,20},{14,22},{1,9},{3... | collective-permute-start | bytes 196616 | tf_op jit(solution)/shard_map/ppermute | solution.py:122
  673.0 53.3 %collective-permute-start.87 = (bf16[1,1,1,32,3072]{4,3,2,1,0:T(8,128)(2,1)}, bf16[1,1,1,32,3072]{4,3,2,1,0:T(8,128)(2,1)}, u32[]{:S(2)}, u32[]{:S(2)}) collective-permute-start(bf16[1,1,1,32,3072]{4,3,2,1,0:T(8,128)(2,1)} %get-tuple-element.224), channel_id=1, source_target_pairs={{0,8},{2,10},{4,12},{6,14},{8,16},{10,18},{12,20},{14,22},{16,24},... | collective-permute-start | bytes 589832 | tf_op jit(solution)/shard_map/ppermute | solution.py:122
  678.2 23.6 %collective-permute-start.71 = (bf16[1,1,1,32,1024]{4,3,2,1,0:T(8,128)(2,1)}, bf16[1,1,1,32,1024]{4,3,2,1,0:T(8,128)(2,1)}, u32[]{:S(2)}, u32[]{:S(2)}) collective-permute-start(bf16[1,1,1,32,1024]{4,3,2,1,0:T(8,128)(2,1)} %get-tuple-element.256), channel_id=1, source_target_pairs={{0,8},{2,10},{4,12},{6,14},{8,16},{10,18},{12,20},{14,22},{16,24},... | collective-permute-start | bytes 196616 | tf_op jit(solution)/shard_map/ppermute | solution.py:122
  692.1 14.3 %collective-permute-start.74 = (bf16[1,1,1,32,1024]{4,3,2,1,0:T(8,128)(2,1)}, bf16[1,1,1,32,1024]{4,3,2,1,0:T(8,128)(2,1)}, u32[]{:S(2)}, u32[]{:S(2)}) collective-permute-start(bf16[1,1,1,32,1024]{4,3,2,1,0:T(8,128)(2,1)} %add_convert_fusion.41), channel_id=1, source_target_pairs={{8,0},{10,2},{12,4},{14,6},{16,8},{18,10},{20,12},{22,14},{24,16},... | collective-permute-start | bytes 196616 | tf_op jit(solution)/shard_map/ppermute | solution.py:125
  708.6 35.3 %collective-permute-start.95 = (bf16[1,1,1,32,3072]{4,3,2,1,0:T(8,128)(2,1)}, bf16[1,1,1,32,3072]{4,3,2,1,0:T(8,128)(2,1)S(1)}, u32[]{:S(2)}, u32[]{:S(2)}) collective-permute-start(bf16[1,1,1,32,3072]{4,3,2,1,0:T(8,128)(2,1)} %get-tuple-element.228), channel_id=1, source_target_pairs={{0,8},{2,10},{4,12},{6,14},{8,16},{10,18},{12,20},{14,22},{16,24},... | collective-permute-start | bytes 589832 | tf_op jit(solution)/shard_map/ppermute | solution.py:122
  725.0 8.0 collective-permute-start.90
  726.3 19.0 %collective-permute-start.98 = (bf16[1,1,1,32,3072]{4,3,2,1,0:T(8,128)(2,1)}, bf16[1,1,1,32,3072]{4,3,2,1,0:T(8,128)(2,1)S(1)}, u32[]{:S(2)}, u32[]{:S(2)}) collective-permute-start(bf16[1,1,1,32,3072]{4,3,2,1,0:T(8,128)(2,1)} %add_convert_fusion.16), channel_id=1, source_target_pairs={{8,0},{10,2},{12,4},{14,6},{16,8},{18,10},{20,12},{22,14},{24,16},... | collective-permute-start | bytes 589832 | tf_op jit(solution)/shard_map/ppermute | solution.py:125
  734.8 11.5 %collective-permute-start.43 = (f32[1,2,2,8,128]{4,3,2,1,0:T(8,128)S(1)}, f32[1,2,2,8,128]{4,3,2,1,0:T(8,128)S(1)}, u32[]{:S(2)}, u32[]{:S(2)}) collective-permute-start(f32[1,2,2,8,128]{4,3,2,1,0:T(8,128)S(1)} %get-tuple-element.266), channel_id=1, source_target_pairs={{0,8},{2,10},{4,12},{6,14},{8,16},{10,18},{12,20},{14,22},{16,24},... | collective-permute-start | bytes 49160 | tf_op jit(solution)/shard_map/ppermute | solution.py:122
  763.3 15.5 %collective-permute-start.51 = (bf16[4,1,1,32,2304]{4,3,2,1,0:T(8,128)(2,1)S(1)}, bf16[4,1,1,32,2304]{4,3,2,1,0:T(8,128)(2,1)S(1)}, u32[]{:S(2)}, u32[]{:S(2)}) collective-permute-start(bf16[4,1,1,32,2304]{4,3,2,1,0:T(8,128)(2,1)S(1)} %constant_dynamic-slice_fusion.24), channel_id=1, source_target_pairs={{0,4},{2,6},{4,0},{6,2},{8,12},{10,14},{12,8},{14,10},{16,20},{18,... | collective-permute-start | bytes 1769480 | tf_op jit(solution)/shard_map/ppermute | solution.py:111
  765.7 17.7 %collective-permute-start.59 = (bf16[4,1,1,32,2304]{4,3,2,1,0:T(8,128)(2,1)S(1)}, bf16[4,1,1,32,2304]{4,3,2,1,0:T(8,128)(2,1)S(1)}, u32[]{:S(2)}, u32[]{:S(2)}) collective-permute-start(bf16[4,1,1,32,2304]{4,3,2,1,0:T(8,128)(2,1)S(1)} %constant_dynamic-slice_fusion.20), channel_id=1, source_target_pairs={{0,2},{2,0},{4,6},{6,4},{8,10},{10,8},{12,14},{14,12},{16,18},{18,... | collective-permute-start | bytes 1769480 | tf_op jit(solution)/shard_map/ppermute | solution.py:111
  782.7 10.6 %collective-permute-start.55 = (bf16[1,1,1,32,2304]{4,3,2,1,0:T(8,128)(2,1)S(1)}, bf16[1,1,1,32,2304]{4,3,2,1,0:T(8,128)(2,1)S(1)}, u32[]{:S(2)}, u32[]{:S(2)}) collective-permute-start(bf16[1,1,1,32,2304]{4,3,2,1,0:T(8,128)(2,1)S(1)} %get-tuple-element.237), channel_id=1, source_target_pairs={{24,16},{26,18},{28,20},{30,22},{25,17},{27,19},{29,21},{31,23}} | collective-permute-start | bytes 442376 | tf_op jit(solution)/shard_map/ppermute | solution.py:125
  784.9 15.8 %collective-permute-start.63 = (bf16[1,1,1,32,2304]{4,3,2,1,0:T(8,128)(2,1)S(1)}, bf16[1,1,1,32,2304]{4,3,2,1,0:T(8,128)(2,1)S(1)}, u32[]{:S(2)}, u32[]{:S(2)}) collective-permute-start(bf16[1,1,1,32,2304]{4,3,2,1,0:T(8,128)(2,1)S(1)} %get-tuple-element.241), channel_id=1, source_target_pairs={{24,16},{26,18},{28,20},{30,22},{25,17},{27,19},{29,21},{31,23}} | collective-permute-start | bytes 442376 | tf_op jit(solution)/shard_map/ppermute | solution.py:125
  786.5 8.4 %collective-permute-start.53 = (bf16[1,1,1,32,2304]{4,3,2,1,0:T(8,128)(2,1)S(1)}, bf16[1,1,1,32,2304]{4,3,2,1,0:T(8,128)(2,1)S(1)}, u32[]{:S(2)}, u32[]{:S(2)}) collective-permute-start(bf16[1,1,1,32,2304]{4,3,2,1,0:T(8,128)(2,1)S(1)} %add_convert_fusion.34), channel_id=1, source_target_pairs={{0,8},{2,10},{4,12},{6,14},{8,16},{10,18},{12,20},{14,22},{1,9},{3... | collective-permute-start | bytes 442376 | tf_op jit(solution)/shard_map/ppermute | solution.py:122
  790.9 9.8 %collective-permute-start.61 = (bf16[1,1,1,32,2304]{4,3,2,1,0:T(8,128)(2,1)S(1)}, bf16[1,1,1,32,2304]{4,3,2,1,0:T(8,128)(2,1)S(1)}, u32[]{:S(2)}, u32[]{:S(2)}) collective-permute-start(bf16[1,1,1,32,2304]{4,3,2,1,0:T(8,128)(2,1)S(1)} %add_convert_fusion.29), channel_id=1, source_target_pairs={{0,8},{2,10},{4,12},{6,14},{8,16},{10,18},{12,20},{14,22},{1,9},{3... | collective-permute-start | bytes 442376 | tf_op jit(solution)/shard_map/ppermute | solution.py:122
  795.0 11.7 %collective-permute-start.56 = (bf16[1,1,1,32,2304]{4,3,2,1,0:T(8,128)(2,1)S(1)}, bf16[1,1,1,32,2304]{4,3,2,1,0:T(8,128)(2,1)S(1)}, u32[]{:S(2)}, u32[]{:S(2)}) collective-permute-start(bf16[1,1,1,32,2304]{4,3,2,1,0:T(8,128)(2,1)S(1)} %get-tuple-element.235), channel_id=1, source_target_pairs={{16,8},{18,10},{20,12},{22,14},{24,16},{26,18},{28,20},{30,22},{17... | collective-permute-start | bytes 442376 | tf_op jit(solution)/shard_map/ppermute | solution.py:125
  795.7 13.7 %collective-permute-start.54 = (bf16[1,1,1,32,2304]{4,3,2,1,0:T(8,128)(2,1)S(1)}, bf16[1,1,1,32,2304]{4,3,2,1,0:T(8,128)(2,1)S(1)}, u32[]{:S(2)}, u32[]{:S(2)}) collective-permute-start(bf16[1,1,1,32,2304]{4,3,2,1,0:T(8,128)(2,1)S(1)} %get-tuple-element.234), channel_id=1, source_target_pairs={{0,8},{2,10},{4,12},{6,14},{8,16},{10,18},{12,20},{14,22},{16,24},... | collective-permute-start | bytes 442376 | tf_op jit(solution)/shard_map/ppermute | solution.py:122
  801.5 13.0 %collective-permute-start.62 = (bf16[1,1,1,32,2304]{4,3,2,1,0:T(8,128)(2,1)S(1)}, bf16[1,1,1,32,2304]{4,3,2,1,0:T(8,128)(2,1)S(1)}, u32[]{:S(2)}, u32[]{:S(2)}) collective-permute-start(bf16[1,1,1,32,2304]{4,3,2,1,0:T(8,128)(2,1)S(1)} %get-tuple-element.238), channel_id=1, source_target_pairs={{0,8},{2,10},{4,12},{6,14},{8,16},{10,18},{12,20},{14,22},{16,24},... | collective-permute-start | bytes 442376 | tf_op jit(solution)/shard_map/ppermute | solution.py:122
  808.1 9.0 %collective-permute-start.65 = (bf16[1,1,1,32,2304]{4,3,2,1,0:T(8,128)(2,1)S(1)}, bf16[1,1,1,32,2304]{4,3,2,1,0:T(8,128)(2,1)S(1)}, u32[]{:S(2)}, u32[]{:S(2)}) collective-permute-start(bf16[1,1,1,32,2304]{4,3,2,1,0:T(8,128)(2,1)S(1)} %add_convert_fusion.26), channel_id=1, source_target_pairs={{8,0},{10,2},{12,4},{14,6},{16,8},{18,10},{20,12},{22,14},{24,16},... | collective-permute-start | bytes 442376 | tf_op jit(solution)/shard_map/ppermute | solution.py:125
  (227 other events, 2623.6 us)
